TPU v7x, 32 devices: a whole 2x2x4 slice. The times are simulated.
32 devices in a mesh: groups: 2 (over x), seq: 16 (over z, y, core).
Axes of the slice: x: 2, y: 2, z: 4, core: 2. Of those that a mesh axis runs over, the one named last changes fastest.
Arguments:
- query_rows: bfloat16 [6144, 2048], P(('groups', 'seq')), parts along dimension 0, may hold values from -5.5 to 5.5, as said below
- key_rows: bfloat16 [6144, 2048], P(('groups', 'seq')), parts along dimension 0, may hold values from -5.5 to 5.5, as said below
- value_rows: bfloat16 [6144, 2048], P(('groups', 'seq')), parts along dimension 0, may hold values from -6 to 6
- out_grad: bfloat16 [6144, 2048], P(('groups', 'seq')), parts along dimension 0, may hold values from -6 to 6
Outputs:
- attended: bfloat16 [6144, 2048], P(('groups', 'seq')), parts along dimension 0
- query_grad: bfloat16 [6144, 2048], P(('groups', 'seq')), parts along dimension 0
- key_grad: bfloat16 [6144, 2048], P(('groups', 'seq')), parts along dimension 0
- value_grad: bfloat16 [6144, 2048], P(('groups', 'seq')), parts along dimension 0
There are 2 independent parts, one for each index of `groups`. A program takes and returns all parts, laid end to end along the dimension named above; each array names one. Nothing has to cross between parts.
Inputs may be any that keep to these rules, and one draw needn't show every extreme that they name: `query_rows`: queries of order one. `key_rows`: keys of order one.
All inputs are finite; a program needn't handle non-finite values.
Results may differ from a plain program's by a relative error of at most 0.017.
Values may be sent and summed in bfloat16 or wider, within the bound.
A program may use at most 128 MiB of HBM per device.

v0:
```python
import math

import jax
import jax.numpy as jnp
from jax import lax
from jax.sharding import PartitionSpec as P

HEADS = 16
HEAD_DIM = 128
BLOCK = 128
HALO = 64
OFF = 32
TAIL = 96
SLOT_DEV = 2


def shifted(block, axis, distance):
    devices = range(lax.axis_size(axis))
    route = [(i - distance, i) for i in devices if i - distance in devices]
    return lax.ppermute(block, axis, route)


def body(query_rows, key_rows, value_rows, out_grad):
    rows = query_rows.shape[0]
    feats = query_rows.shape[1]
    scale = 1.0 / math.sqrt(HEAD_DIM)
    shard = lax.axis_index("seq")
    shards = lax.axis_size("seq")
    first = shard * rows
    lead = (first + OFF) % BLOCK
    window = rows + BLOCK + HALO
    nblocks = window // BLOCK
    filler_rows = BLOCK + HALO - OFF
    tails = jnp.stack([key_rows[rows - TAIL :], value_rows[rows - TAIL :]])
    before = shifted(tails, "seq", 1)

    def framed(own, prior):
        filler = jnp.zeros((filler_rows, own.shape[1]), own.dtype)
        whole = jnp.concatenate([prior, own, filler], axis=0)
        return lax.dynamic_slice_in_dim(whole, TAIL - lead, window, 0)

    def unframed(whole):
        return lax.dynamic_slice_in_dim(whole, lead, rows, 0)

    offset = BLOCK - 1 - lead
    slot_index = offset + BLOCK * jnp.arange(SLOT_DEV, dtype=jnp.int32)
    slot_live = slot_index < rows
    clipped = jnp.minimum(slot_index, rows - 1)
    own_slots = jnp.stack([key_rows[clipped], value_rows[clipped]])
    own_slots = jnp.where(slot_live[None, :, None], own_slots, jnp.zeros((), jnp.bfloat16))
    all_slots = lax.all_gather(own_slots, "seq", axis=1, tiled=True)
    slot_count = shards * SLOT_DEV
    slot_ids = jnp.arange(slot_count, dtype=jnp.int32)
    owner = slot_ids // SLOT_DEV
    owner_offset = BLOCK - 1 - (owner * rows + OFF) % BLOCK + BLOCK * (slot_ids % SLOT_DEV)
    slot_pos = owner * rows + owner_offset
    slot_valid = owner_offset < rows
    frame_idx = jnp.arange(window, dtype=jnp.int32)
    row_valid = (frame_idx >= lead) & (frame_idx < lead + rows)
    frame_pos = first - lead + frame_idx
    key_valid = frame_pos >= 0
    frame_block = (frame_pos + OFF) // BLOCK
    row_mask = row_valid.reshape(nblocks, BLOCK)
    key_mask = key_valid.reshape(nblocks, BLOCK)
    causal = jnp.tril(jnp.ones((BLOCK, BLOCK), dtype=bool))
    local_ok = (causal[None, :, :] & row_mask[:, :, None] & key_mask[:, None, :])[None]
    summary_ok = (
        slot_valid[None, :]
        & ((slot_pos[None, :] + OFF) // BLOCK < frame_block[:, None])
        & row_valid[:, None]
    )
    summary_ok = summary_ok.reshape(nblocks, BLOCK, slot_count)[None]
    zero_prior = jnp.zeros((TAIL, feats), jnp.bfloat16)
    q_frame = framed(query_rows, zero_prior).reshape(nblocks, BLOCK, HEADS, HEAD_DIM)
    g_frame = framed(out_grad, zero_prior).reshape(nblocks, BLOCK, HEADS, HEAD_DIM)
    k_frame = framed(key_rows, before[0]).reshape(nblocks, BLOCK, HEADS, HEAD_DIM)
    v_frame = framed(value_rows, before[1]).reshape(nblocks, BLOCK, HEADS, HEAD_DIM)
    k_slots = all_slots[0].reshape(slot_count, HEADS, HEAD_DIM)
    v_slots = all_slots[1].reshape(slot_count, HEADS, HEAD_DIM)
    local_scores = (
        jnp.einsum("nihd,njhd->hnij", q_frame, k_frame, preferred_element_type=jnp.float32) * scale
    )
    summary_scores = (
        jnp.einsum("nihd,shd->hnis", q_frame, k_slots, preferred_element_type=jnp.float32) * scale
    )
    top = jnp.maximum(
        jnp.max(jnp.where(local_ok, local_scores, -jnp.inf), axis=-1),
        jnp.max(jnp.where(summary_ok, summary_scores, -jnp.inf), axis=-1),
    )
    top = jnp.where(row_mask[None], top, 0.0)
    local_exp = jnp.where(local_ok, jnp.exp(local_scores - top[..., None]), 0.0)
    summary_exp = jnp.where(summary_ok, jnp.exp(summary_scores - top[..., None]), 0.0)
    total = jnp.sum(local_exp, axis=-1) + jnp.sum(summary_exp, axis=-1)
    total = jnp.where(row_mask[None], total, 1.0)
    local_prob = local_exp / total[..., None]
    summary_prob = summary_exp / total[..., None]
    local_weights = local_prob.astype(jnp.bfloat16)
    summary_weights = summary_prob.astype(jnp.bfloat16)
    out_frame = (
        jnp.einsum("hnij,njhd->nihd", local_weights, v_frame, preferred_element_type=jnp.float32)
        + jnp.einsum("hnis,shd->nihd", summary_weights, v_slots, preferred_element_type=jnp.float32)
    ).astype(jnp.bfloat16)
    delta = jnp.sum(g_frame.astype(jnp.float32) * out_frame.astype(jnp.float32), axis=-1)
    delta = jnp.transpose(delta, (2, 0, 1))[..., None]
    local_dw = jnp.einsum("nihd,njhd->hnij", g_frame, v_frame, preferred_element_type=jnp.float32)
    summary_dw = jnp.einsum("nihd,shd->hnis", g_frame, v_slots, preferred_element_type=jnp.float32)
    local_ds = (local_prob * (local_dw - delta)).astype(jnp.bfloat16)
    summary_ds = (summary_prob * (summary_dw - delta)).astype(jnp.bfloat16)
    qgrad_frame = scale * (
        jnp.einsum("hnij,njhd->nihd", local_ds, k_frame, preferred_element_type=jnp.float32)
        + jnp.einsum("hnis,shd->nihd", summary_ds, k_slots, preferred_element_type=jnp.float32)
    )
    key_window = jnp.einsum(
        "hnij,nihd->njhd", local_ds, q_frame, preferred_element_type=jnp.float32
    ).reshape(window, feats)
    value_window = jnp.einsum(
        "hnij,nihd->njhd", local_weights, g_frame, preferred_element_type=jnp.float32
    ).reshape(window, feats)
    head_terms = jnp.stack([key_window[:TAIL], value_window[:TAIL]])
    spaced = jnp.concatenate([jnp.zeros_like(head_terms), head_terms], axis=1)
    tail_terms = lax.dynamic_slice_in_dim(spaced, lead, TAIL, 1)
    after = shifted(tail_terms, "seq", -1)
    key_sum = unframed(key_window).at[rows - TAIL :].add(after[0])
    value_sum = unframed(value_window).at[rows - TAIL :].add(after[1])
    key_part = jnp.einsum(
        "hnis,nihd->shd", summary_ds, q_frame, preferred_element_type=jnp.float32
    ).reshape(slot_count, feats)
    value_part = jnp.einsum(
        "hnis,nihd->shd", summary_weights, g_frame, preferred_element_type=jnp.float32
    ).reshape(slot_count, feats)
    mine = lax.psum_scatter(
        jnp.concatenate([key_part, value_part], axis=1), "seq", scatter_dimension=0, tiled=True
    )
    live = slot_live[:, None]
    key_sum = key_sum.at[clipped].add(jnp.where(live, mine[:, :feats], 0.0))
    value_sum = value_sum.at[clipped].add(jnp.where(live, mine[:, feats:], 0.0))
    attended = unframed(out_frame.reshape(window, feats))
    query_grad = unframed(qgrad_frame.astype(jnp.bfloat16).reshape(window, feats))
    return (
        attended,
        query_grad,
        (scale * key_sum).astype(jnp.bfloat16),
        value_sum.astype(jnp.bfloat16),
    )


def solution(mesh):
    return jax.shard_map(
        body,
        mesh=mesh,
        in_specs=(
            P(("groups", "seq"), None),
            P(("groups", "seq"), None),
            P(("groups", "seq"), None),
            P(("groups", "seq"), None),
        ),
        out_specs=(
            P(("groups", "seq"), None),
            P(("groups", "seq"), None),
            P(("groups", "seq"), None),
            P(("groups", "seq"), None),
        ),
        check_vma=False,
    )
```

profile of v0, /device:TPU:1, one launch (start us, length us, event | category | flops | bytes accessed | tf_op | source)
XLA Modules:
  0.0 183.8 jit_solution(4242354472508319320)
XLA Ops:
  7.2 1.3 slice_bitcast_fusion.6
  8.5 0.9 pad_maximum_fusion
  9.5 4.5 %collective-permute-start = (bf16[2,96,2048]{2,1,0:T(8,128)(2,1)}, bf16[2,96,2048]{2,1,0:T(8,128)(2,1)}, u32[]{:S(2)}, u32[]{:S(2)}) collective-permute-start(bf16[2,96,2048]{2,1,0:T(8,128)(2,1)} %pad_maximum_fusion), channel_id=1, source_target_pairs={{0,1},{1,2},{2,3},{3,4},{4,5},{5,6},{6,7},{7,8},{8,9},{9,10},{10,1... | collective-permute-start | bytes 2359304 | tf_op jit(solution)/shard_map/ppermute | solution.py:20
  14.1 0.5 copy-done.23
  14.6 0.6 gather_fusion
  15.1 0.6 gather_fusion.1
  15.8 0.1 broadcast_select_fusion
  15.9 21.8 %all_gather.3 = bf16[2,32,2048]{2,0,1:T(2,128)(2,1)S(1)} all-gather(bf16[2,2,2048]{2,0,1:T(2,128)(2,1)S(1)} %copy.53), channel_id=1, replica_groups=mesh['groups'=2,'seq'=16] {'seq'}, dimensions={1}, use_global_device_ids=true | all-gather | bytes 278528 | tf_op jit(solution)/shard_map/all_gather | solution.py:51
  37.8 1.1 slice_reduce_fusion
  38.9 0.7 copy.111
  39.6 0.6 dynamic-slice.22
  40.8 0.1 pad_dynamic-slice_fusion.8
  40.9 0.1 and_and_fusion.1
  41.0 0.1 and_and_fusion
  41.2 1.2 slice_bitcast_fusion.4
  42.3 4.7 %fusion.7 = (bf16[48,8,16,128]{3,1,2,0:T(8,128)(2,1)S(1)}, bf16[48,8,16,128]{3,1,2,0:T(8,128)(2,1)S(1)}, bf16[48,8,16,128]{3,1,2,0:T(8,128)(2,1)}, bf16[48,8,16,128]{3,1,2,0:T(8,128)(2,1)S(1)}) fusion(s32[]{:T(128)S(6)} %select_n.141, bf16[192,2048]{1,0:T(8,128)(2,1)S(1)} %copy-done.20, bf16[384]{0:T(512)(128)(2,1)S(1)} %get-tuple-element.44, ...), kind=kLoop, calls=%fused_computation.29 | loop fusion | flops 15728640 | bytes 10225156
  47.0 0.4 copy.106
  47.4 0.4 copy.107
  47.8 1.8 select_reduce_fusion
  49.6 0.8 select_reduce_fusion.1
  50.5 0.2 fusion.53
  50.7 0.8 fusion.4
  51.5 0.4 copy.110
  52.0 2.0 %fusion.54 = bf16[16,3,128,128]{2,3,1,0:T(8,128)(2,1)} fusion(f32[16,3,128]{2,1,0:T(4,128)S(1)} %add_select_fusion, f32[16,3,128]{2,1,0:T(4,128)S(1)} %maximum_select_fusion, f32[16,3,128,128]{2,3,1,0:T(8,128)S(1)} %get-tuple-element.39, pred[3,128,128]{1,2,0:T(8,128)(4,1)S(1)} %and_and_fusion), kind=kLoop, calls=%fused_computation.86 | loop fusion | flops 3932160 | bytes 4816896 | tf_op jit(solution)/shard_map/convert_element_type | solution.py:97
  54.0 1.4 fusion.45
  55.4 2.3 %copy.63 = bf16[3,128,16,128]{1,3,2,0:T(8,128)(2,1)S(1)} copy(bf16[3,128,16,128]{3,2,1,0:T(8,128)(2,1)} %bitcast.150) | data formatting | bytes 3145728 | tf_op jit(solution)/shard_map/reshape | solution.py:75
  57.7 1.0 copy.187
  58.7 1.9 %copy.105 = bf16[48,8,16,128]{3,2,1,0:T(8,128)(2,1)S(1)} copy(bf16[48,8,16,128]{3,1,2,0:T(8,128)(2,1)} %get-tuple-element.36) | data formatting | bytes 3145728
  60.6 0.7 fusion.24
  61.3 2.9 %convolution_bitcast_fusion = f32[3,128,16,128]{1,3,2,0:T(8,128)} fusion(bf16[3,128,16,128]{1,3,2,0:T(8,128)(2,1)S(1)} %copy.63, bf16[16,3,128,128]{2,3,1,0:T(8,128)(2,1)S(1)} %copy-done), kind=kOutput, calls=%fused_computation.19 | convolution fusion | flops 201326592 | bytes 6291456 | tf_op jit(solution)/shard_map/hnij,nihd->njhd/dot_general | solution.py:116
  64.2 2.1 %multiply_reduce_fusion = (f32[3,128,16]{1,2,0:T(8,128)S(1)}, bf16[3,128,16,128]{1,3,2,0:T(8,128)(2,1)}) fusion(bf16[3,128,16,128]{1,3,2,0:T(8,128)(2,1)S(1)} %copy.63, f32[3,16,128,128]{3,2,1,0:T(8,128)S(1)} %fusion.24, bf16[32,2048]{1,0:T(8,128)(2,1)S(1)} %get-tuple-element.28, f32[16,3,128]{2,1,0:T(4,128)S(1)} %add_select_fusion, ...), kind=kOutput, calls=%fused_computation.14 | convolution fusion | flops 55830528 | bytes 7294976 | tf_op jit(solution)/shard_map/hnis,shd->nihd/dot_general | solution.py:101
  66.4 0.7 copy-done.6
  67.1 2.3 %multiply_convert_fusion = bf16[16,3,128,128]{2,3,1,0:T(8,128)(2,1)S(1)} fusion(bf16[3,128,16,128]{3,2,1,0:T(8,128)(2,1)S(1)} %bitcast.158, f32[16,3,128]{2,1,0:T(4,128)S(1)} %copy.64, bf16[3,128,16,128]{3,2,1,0:T(8,128)(2,1)S(1)} %bitcast.151, f32[16,3,128]{2,1,0:T(4,128)S(1)} %add_select_fusion, f32[16,3,128]{2,1,0:T(4,128)S(1)} %maximum_select_fusion, ...), kind=kOutput, calls=%fused_computation.13 | convolution fusion | flops 206831616 | bytes 7987200 | tf_op jit(solution)/shard_map/nihd,njhd->hnij/dot_general | solution.py:105
  69.5 1.7 fusion.33
  71.1 0.6 fusion.42
  71.7 0.8 pad_maximum_fusion.1
  72.6 2.9 %convolution_bitcast_fusion.1 = f32[3,128,16,128]{1,3,2,0:T(8,128)} fusion(bf16[3,128,16,128]{3,2,1,0:T(8,128)(2,1)S(1)} %bitcast.140, bf16[16,3,128,128]{2,3,1,0:T(8,128)(2,1)S(1)} %multiply_convert_fusion), kind=kOutput, calls=%fused_computation.20 | convolution fusion | flops 201326592 | bytes 6291456 | tf_op jit(solution)/shard_map/hnij,nihd->njhd/dot_general | solution.py:113
  75.5 3.6 %copy.76 = f32[3,128,16,128]{3,2,1,0:T(8,128)} copy(f32[3,128,16,128]{1,3,2,0:T(8,128)} %convolution_bitcast_fusion.1) | data formatting | bytes 6291456 | tf_op jit(solution)/shard_map/hnij,nihd->njhd/transpose | solution.py:113
  79.1 3.3 %copy.184 = f32[48,8,16,128]{3,1,2,0:T(8,128)S(1)} copy(f32[48,8,16,128]{3,2,1,0:T(8,128)} %bitcast.147) | data formatting | bytes 6291456
  82.5 0.9 slice_bitcast_fusion.3
  83.4 3.6 %copy.79 = f32[3,128,16,128]{3,2,1,0:T(8,128)} copy(f32[3,128,16,128]{1,3,2,0:T(8,128)} %convolution_bitcast_fusion) | data formatting | bytes 6291456 | tf_op jit(solution)/shard_map/hnij,nihd->njhd/transpose | solution.py:116
  87.0 3.3 %copy.183 = f32[48,8,16,128]{3,1,2,0:T(8,128)S(1)} copy(f32[48,8,16,128]{3,2,1,0:T(8,128)} %bitcast.148) | data formatting | bytes 6291456
  90.3 0.1 slice_bitcast_fusion.2
  90.4 1.6 copy-done.14
  92.0 1.5 fusion.18
  93.5 2.6 %collective-permute-start.1 = (f32[2,96,2048]{2,1,0:T(8,128)}, f32[2,96,2048]{2,1,0:T(8,128)}, u32[]{:S(2)}, u32[]{:S(2)}) collective-permute-start(f32[2,96,2048]{2,1,0:T(8,128)} %fusion.18), channel_id=1, source_target_pairs={{1,0},{2,1},{3,2},{4,3},{5,4},{6,5},{7,6},{8,7},{9,8},{10,9},{11,1... | collective-permute-start | bytes 4718600 | tf_op jit(solution)/shard_map/ppermute | solution.py:20
  96.1 0.7 fusion.21
  96.8 1.8 fusion.1
  98.6 2.9 %copy.73 = bf16[3,128,16,128]{3,2,1,0:T(8,128)(2,1)} copy(bf16[3,128,16,128]{1,3,2,0:T(8,128)(2,1)} %fusion.1) | data formatting | bytes 3145728 | tf_op jit(solution)/shard_map/convert_element_type | solution.py:138
  101.5 3.0 %copy.185 = bf16[48,8,16,128]{3,1,2,0:T(8,128)(2,1)} copy(bf16[48,8,16,128]{3,2,1,0:T(8,128)(2,1)} %bitcast.153) | data formatting | bytes 3145728
  104.5 2.9 %copy.60 = bf16[3,128,16,128]{3,2,1,0:T(8,128)(2,1)} copy(bf16[3,128,16,128]{1,3,2,0:T(8,128)(2,1)} %get-tuple-element.43) | data formatting | bytes 3145728 | tf_op jit(solution)/shard_map/convert_element_type | solution.py:102
  107.4 1.9 %copy.186 = bf16[48,8,16,128]{3,1,2,0:T(8,128)(2,1)S(1)} copy(bf16[48,8,16,128]{3,2,1,0:T(8,128)(2,1)} %bitcast.154) | data formatting | bytes 3145728
  109.4 1.1 constant_dynamic-slice_fusion.2
  110.5 1.1 constant_dynamic-slice_fusion.3
  111.5 1.4 constant_dynamic-slice_fusion.1
  112.9 1.1 copy-done.2
  114.0 1.4 constant_dynamic-slice_fusion
  115.4 0.9 collective-permute-done.1
  116.2 2.8 %fusion.49 = (f32[192,2048]{1,0:T(8,128)}, f32[192,2048]{1,0:T(8,128)}) fusion(f32[192,2048]{1,0:T(8,128)} %constant_dynamic-slice_fusion, f32[2,96,2048]{2,1,0:T(8,128)} %collective-permute-done.1, f32[384,2048]{1,0:T(8,128)S(1)} %bitcast.146, s32[]{:T(128)S(6)} %dynamic_slice.36, f32[192,2048]{1,0:T(8,128)} %constant_dynamic-slice_fusion.1, ...), kind=kLoop, calls=%fused_computation.74 | loop fusion | flops 393216 | bytes 4718596 | tf_op jit(solution)/shard_map/scatter-add | solution.py:124
  119.0 46.0 %all-reduce.4.cloned.1.call-done = f32[32,4096]{1,0:T(8,128)} async-done(((f32[32,4096]{1,0:T(8,128)}), f32[32,4096]{1,0:T(8,128)}) %all-reduce.4.cloned.1.call-update) | async-done | bytes 524304
  165.1 3.5 %scatter_custom_fusion.1 = f32[192,2048]{1,0:T(8,128)} fusion(f32[192,2048]{1,0:T(8,128)} %get-tuple-element.30, s32[2]{0:T(128)} %copy-done.23, f32[32,4096]{1,0:T(8,128)} %all-reduce.4.cloned.1.call-done, u32[]{:T(128)S(6)} %multiply.20, u32[]{:T(128)S(6)} %convert.2, pred[2]{0:T(512)(128)(4,1)S(1)} %add_compare_fusion.1, f32[]{:T(128)} %constant.190.clone.1), kind=kCustom, calls=%fused_computation.111 | custom fusion | flops 8192 | bytes 1589770 | tf_op jit(solution)/shard_map/scatter-add | solution.py:136
  168.6 2.4 %convert_element_type.39 = bf16[192,2048]{1,0:T(8,128)(2,1)} convert(f32[192,2048]{1,0:T(8,128)} %scatter_custom_fusion.1) | non-fusion elementwise | flops 393216 | bytes 2359296 | tf_op jit(solution)/shard_map/convert_element_type | solution.py:143
  171.0 3.5 %scatter_custom_fusion = f32[192,2048]{1,0:T(8,128)} fusion(f32[192,2048]{1,0:T(8,128)} %get-tuple-element.31, s32[2]{0:T(128)} %copy-done.23, f32[32,4096]{1,0:T(8,128)} %all-reduce.4.cloned.1.call-done, u32[]{:T(128)S(6)} %multiply.20, u32[]{:T(128)} %constant.195, pred[2]{0:T(512)(128)(4,1)S(1)} %add_compare_fusion.1, f32[]{:T(128)} %constant.190.clone.1), kind=kCustom, calls=%fused_computation.113 | custom fusion | flops 8192 | bytes 1590278 | tf_op jit(solution)/shard_map/scatter-add | solution.py:135
  174.5 2.4 %multiply_convert_fusion.1 = bf16[192,2048]{1,0:T(8,128)(2,1)} fusion(f32[192,2048]{1,0:T(8,128)} %scatter_custom_fusion), kind=kLoop, calls=%fused_computation.53 | loop fusion | flops 786432 | bytes 2359296 | tf_op jit(solution)/shard_map/convert_element_type | solution.py:142
  (65 shorter events, 0.4 us)
Async XLA Ops:
  7.2 8.0 %copy-start.15 = (bf16[192,2048]{1,0:T(8,128)(2,1)S(1)}, bf16[192,2048]{1,0:T(8,128)(2,1)}, u32[]{:S(2)}) copy-start(bf16[192,2048]{1,0:T(8,128)(2,1)} %param.10) | copy-start | bytes 2359300
  7.2 7.4 %copy-start.16 = (bf16[192,2048]{1,0:T(8,128)(2,1)S(1)}, bf16[192,2048]{1,0:T(8,128)(2,1)}, u32[]{:S(2)}) copy-start(bf16[192,2048]{1,0:T(8,128)(2,1)} %param.9) | copy-start | bytes 2359300
  7.2 157.9 %all-reduce.4.cloned.1.call-start = ((), (), s32[]{:S(2)}) async-start(), calls=%async_computation | async-start | bytes 1048576
  8.5 31.0 %copy-start.24 = (u32[32]{0:T(128)S(1)}, u32[32]{0:T(128)}, u32[]{:S(2)}) copy-start(u32[32]{0:T(128)} %constant.197) | copy-start | bytes 388
  9.5 31.7 %collective-permute-start = (bf16[2,96,2048]{2,1,0:T(8,128)(2,1)}, bf16[2,96,2048]{2,1,0:T(8,128)(2,1)}, u32[]{:S(2)}, u32[]{:S(2)}) collective-permute-start(bf16[2,96,2048]{2,1,0:T(8,128)(2,1)} %pad_maximum_fusion), channel_id=1, source_target_pairs={{0,1},{1,2},{2,3},{3,4},{4,5},{5,6},{6,7},{7,8},{8,9},{9,10},{10,1... | collective-permute-start | bytes 2359304 | tf_op jit(solution)/shard_map/ppermute | solution.py:20
  14.1 0.5 copy-start.23
  37.8 4.6 %copy-start.20 = (bf16[192,2048]{1,0:T(8,128)(2,1)S(1)}, bf16[192,2048]{1,0:T(8,128)(2,1)}, u32[]{:S(2)}) copy-start(bf16[192,2048]{1,0:T(8,128)(2,1)} %param.11) | copy-start | bytes 2359300
  38.8 8.2 %copy-start.17 = (bf16[32,2048]{1,0:T(8,128)(2,1)}, bf16[32,2048]{1,0:T(8,128)(2,1)S(1)}, u32[]{:S(2)}) copy-start(bf16[32,2048]{1,0:T(8,128)(2,1)S(1)} %get-tuple-element.29) | copy-start | bytes 393220
  47.8 1.8 copy-start.7
  49.6 2.3 %copy-start.3 = (f32[16,3,128,128]{2,3,1,0:T(8,128)}, f32[16,3,128,128]{2,3,1,0:T(8,128)S(1)}, u32[]{:S(2)}) copy-start(f32[16,3,128,128]{2,3,1,0:T(8,128)S(1)} %get-tuple-element.39) | copy-start | bytes 9437188
  50.4 3.6 %copy-start.12 = (f32[16,3,128,32]{2,3,1,0:T(8,128)}, f32[16,3,128,32]{2,3,1,0:T(8,128)S(1)}, u32[]{:S(2)}) copy-start(f32[16,3,128,32]{2,3,1,0:T(8,128)S(1)} %get-tuple-element.41) | copy-start | bytes 2359300
  50.5 15.9 %copy-start.19 = (f32[16,3,128]{2,1,0:T(4,128)}, f32[16,3,128]{2,1,0:T(4,128)S(1)}, u32[]{:S(2)}) copy-start(f32[16,3,128]{2,1,0:T(4,128)S(1)} %maximum_select_fusion) | copy-start | bytes 73732
  51.9 2.1 %copy-start.5 = (bf16[48,8,16,128]{3,2,1,0:T(8,128)(2,1)}, bf16[48,8,16,128]{3,2,1,0:T(8,128)(2,1)S(1)}, u32[]{:S(2)}) copy-start(bf16[48,8,16,128]{3,2,1,0:T(8,128)(2,1)S(1)} %copy.110) | copy-start | bytes 4718596
  52.0 14.4 %copy-start.21 = (f32[16,3,128]{2,1,0:T(4,128)}, f32[16,3,128]{2,1,0:T(4,128)S(1)}, u32[]{:S(2)}) copy-start(f32[16,3,128]{2,1,0:T(4,128)S(1)} %add_select_fusion) | copy-start | bytes 73732
  58.7 1.9 %copy-start = (bf16[16,3,128,128]{2,3,1,0:T(8,128)(2,1)S(1)}, bf16[16,3,128,128]{2,3,1,0:T(8,128)(2,1)}, u32[]{:S(2)}) copy-start(bf16[16,3,128,128]{2,3,1,0:T(8,128)(2,1)} %fusion.54) | copy-start | bytes 4718596
  61.3 2.9 %copy-start.13 = (f32[16,3,128,32]{2,3,1,0:T(8,128)S(1)}, f32[16,3,128,32]{2,3,1,0:T(8,128)}, u32[]{:S(2)}) copy-start(f32[16,3,128,32]{2,3,1,0:T(8,128)} %copy-done.12) | copy-start | bytes 2359300
  64.2 2.2 %copy-start.4 = (f32[16,3,128,128]{2,3,1,0:T(8,128)S(1)}, f32[16,3,128,128]{2,3,1,0:T(8,128)}, u32[]{:S(2)}) copy-start(f32[16,3,128,128]{2,3,1,0:T(8,128)} %copy-done.3) | copy-start | bytes 9437188
  64.2 2.9 %copy-start.6 = (bf16[48,8,16,128]{3,2,1,0:T(8,128)(2,1)S(1)}, bf16[48,8,16,128]{3,2,1,0:T(8,128)(2,1)}, u32[]{:S(2)}) copy-start(bf16[48,8,16,128]{3,2,1,0:T(8,128)(2,1)} %copy-done.5) | copy-start | bytes 4718596
  67.1 2.4 %copy-start.22 = (bf16[4,8,16,128]{3,2,1,0:T(8,128)(2,1)S(1)}, bf16[4,8,16,128]{3,2,1,0:T(8,128)(2,1)}, u32[]{:S(2)}) copy-start(bf16[4,8,16,128]{3,2,1,0:T(8,128)(2,1)} %copy.111) | copy-start | bytes 393220
  69.5 3.1 %copy-start.9 = (bf16[16,3,128,128]{2,3,1,0:T(8,128)(2,1)}, bf16[16,3,128,128]{2,3,1,0:T(8,128)(2,1)S(1)}, u32[]{:S(2)}) copy-start(bf16[16,3,128,128]{2,3,1,0:T(8,128)(2,1)S(1)} %multiply_convert_fusion) | copy-start | bytes 4718596
  90.3 3.2 %copy-start.1 = (f32[48,8,16,128]{3,1,2,0:T(8,128)}, f32[48,8,16,128]{3,1,2,0:T(8,128)S(1)}, u32[]{:S(2)}) copy-start(f32[48,8,16,128]{3,1,2,0:T(8,128)S(1)} %copy.183) | copy-start | bytes 9437188
  90.3 1.7 copy-start.14
  92.0 4.1 %copy-start.8 = (bf16[48,8,16,128]{3,2,1,0:T(8,128)(2,1)S(1)}, bf16[48,8,16,128]{3,2,1,0:T(8,128)(2,1)}, u32[]{:S(2)}) copy-start(bf16[48,8,16,128]{3,2,1,0:T(8,128)(2,1)} %copy-done.7) | copy-start | bytes 4718596
  92.0 4.1 %copy-start.10 = (bf16[16,3,128,128]{2,3,1,0:T(8,128)(2,1)S(1)}, bf16[16,3,128,128]{2,3,1,0:T(8,128)(2,1)}, u32[]{:S(2)}) copy-start(bf16[16,3,128,128]{2,3,1,0:T(8,128)(2,1)} %copy-done.9) | copy-start | bytes 4718596
  93.5 3.3 %copy-start.18 = (bf16[32,2048]{1,0:T(8,128)(2,1)S(1)}, bf16[32,2048]{1,0:T(8,128)(2,1)}, u32[]{:S(2)}) copy-start(bf16[32,2048]{1,0:T(8,128)(2,1)} %copy-done.17) | copy-start | bytes 393220
  93.5 22.7 %collective-permute-start.1 = (f32[2,96,2048]{2,1,0:T(8,128)}, f32[2,96,2048]{2,1,0:T(8,128)}, u32[]{:S(2)}, u32[]{:S(2)}) collective-permute-start(f32[2,96,2048]{2,1,0:T(8,128)} %fusion.18), channel_id=1, source_target_pairs={{1,0},{2,1},{3,2},{4,3},{5,4},{6,5},{7,6},{8,7},{9,8},{10,9},{11,1... | collective-permute-start | bytes 4718600 | tf_op jit(solution)/shard_map/ppermute | solution.py:20
  107.4 1.9 %copy-start.11 = (bf16[48,8,16,128]{3,1,2,0:T(8,128)(2,1)S(1)}, bf16[48,8,16,128]{3,1,2,0:T(8,128)(2,1)}, u32[]{:S(2)}) copy-start(bf16[48,8,16,128]{3,1,2,0:T(8,128)(2,1)} %copy.185) | copy-start | bytes 4718596
  111.5 2.5 %copy-start.2 = (f32[48,8,16,128]{3,1,2,0:T(8,128)S(1)}, f32[48,8,16,128]{3,1,2,0:T(8,128)}, u32[]{:S(2)}) copy-start(f32[48,8,16,128]{3,1,2,0:T(8,128)} %copy-done.1) | copy-start | bytes 9437188
Sparse Core Ops, SparseCore 0:
  72.7 92.3 all-reduce.3
where the time goes:
time: 185 us; the launch traced here: 184 us
  local copies, waits for them, and re-layouts  47 us (25%)
  waiting for transfers between devices  46.9 us (25%)
  other arithmetic  26.2 us (14%)
  blocking collectives  21.8 us (12%)
  matrix products  19.6 us (11%)
  between operations  15.2 us (8%)
  starting transfers between devices  7.15 us (4%)
    unnamed x2, waiting for transfers between devices  46 us
    all_gather x1, blocking collectives, body(): all_slots = lax.all_gather(own_slots, 'seq', axis=1, tiled=True)  21.8 us
    unnamed x61, local copies, waits for them, and re-layouts  20 us
    ppermute x2, starting transfers between devices, shifted(): return lax.ppermute(block, axis, route)  7.11 us
    dynamic_slice x4, local copies, waits for them, and re-layouts, unframed(): return lax.dynamic_slice_in_dim(whole, lead, rows, 0)  4.89 us
    unnamed x1, other arithmetic  4.67 us
  transfers between devices with their start and end apart: 3, of which 2 were waited for; matrix products, arithmetic and copies ran while one was open for 24% of the time, Pallas kernels for 0%

commit v1 on v0

v1 whole, which is shorter than its diff:
```python
import functools
import math

import jax
import jax.numpy as jnp
from jax import lax
from jax.experimental import pallas as pl
from jax.experimental.pallas import tpu as pltpu
from jax.sharding import PartitionSpec as P

HEADS = 16
HEAD_DIM = 128
BLOCK = 128
OFF = 32
TAIL = 96
SLOT_DEV = 2
HEADS_STEP = 4
SCALE = 1.0 / math.sqrt(HEAD_DIM)
NEG = -1e30


def shifted(block, axis, distance):
    devices = range(lax.axis_size(axis))
    route = [(i - distance, i) for i in devices if i - distance in devices]
    return lax.ppermute(block, axis, route)


def bias_of(shard, rows, slots):
    first = shard * rows
    shape = (rows, TAIL + rows)
    query = first + lax.broadcasted_iota(jnp.int32, shape, 0)
    pos = first - TAIL + lax.broadcasted_iota(jnp.int32, shape, 1)
    local = (pos >= 0) & (pos <= query) & ((pos + OFF) >> 7 == (query + OFF) >> 7)
    shape = (rows, slots)
    query = first + lax.broadcasted_iota(jnp.int32, shape, 0)
    slot = lax.broadcasted_iota(jnp.int32, shape, 1)
    start = (slot >> 1) * rows
    offset = BLOCK - 1 - ((start + OFF) & (BLOCK - 1)) + BLOCK * (slot & 1)
    summary = (offset < rows) & ((start + offset + OFF) >> 7 < (query + OFF) >> 7)
    return (
        jnp.where(local, 0.0, NEG).astype(jnp.float32),
        jnp.where(summary, 0.0, NEG).astype(jnp.float32),
    )


def dot(a, b, dims):
    return lax.dot_general(a, b, (dims, ((), ())), preferred_element_type=jnp.float32)


NT = ((1,), (1,))
NN = ((1,), (0,))
TN = ((0,), (0,))


def one_head(q, k, v, g, bias):
    scores = dot(q, k, NT) * SCALE + bias
    top = jnp.max(scores, axis=1, keepdims=True)
    expo = jnp.exp(scores - top)
    prob = expo * (1.0 / jnp.sum(expo, axis=1, keepdims=True))
    weights = prob.astype(jnp.bfloat16)
    attended = dot(weights, v, NN).astype(jnp.bfloat16)
    delta = jnp.sum(g.astype(jnp.float32) * attended.astype(jnp.float32), axis=1, keepdims=True)
    dscores = (prob * (dot(g, v, NT) - delta)).astype(jnp.bfloat16)
    qgrad = (dot(dscores, k, NN) * SCALE).astype(jnp.bfloat16)
    return attended, qgrad, dot(dscores, q, TN) * SCALE, dot(weights, g, TN)


def kernel(q_ref, k_ref, v_ref, g_ref, halo_ref, slot_ref, out_ref, qg_ref, kg_ref, vg_ref,
           hg_ref, sg_ref, bias_ref):
    rows = q_ref.shape[0]
    slots = slot_ref.shape[1]

    @pl.when(pl.program_id(0) == 0)
    def _():
        local, summary = bias_of(lax.axis_index("seq"), rows, slots)
        bias_ref[:, : TAIL + rows] = local
        bias_ref[:, TAIL + rows :] = summary

    for h in range(HEADS_STEP):
        c = slice(h * HEAD_DIM, (h + 1) * HEAD_DIM)
        k = jnp.concatenate([halo_ref[0, :, c], k_ref[:, c], slot_ref[0, :, c]], axis=0)
        v = jnp.concatenate([halo_ref[1, :, c], v_ref[:, c], slot_ref[1, :, c]], axis=0)
        attended, qgrad, kg, vg = one_head(q_ref[:, c], k, v, g_ref[:, c], bias_ref[...])
        out_ref[:, c] = attended
        qg_ref[:, c] = qgrad
        for i, (grad, own_ref) in enumerate(((kg, kg_ref), (vg, vg_ref))):
            hg_ref[i, :, c] = grad[:TAIL].astype(jnp.bfloat16)
            own_ref[:, c] = grad[TAIL : TAIL + rows]
            sg_ref[i, :, c] = grad[TAIL + rows :].astype(jnp.bfloat16)


def attention(query_rows, key_rows, value_rows, out_grad, halo, slots):
    rows, feats = query_rows.shape
    count = slots.shape[1]
    wide = HEADS_STEP * HEAD_DIM
    own = pl.BlockSpec((rows, wide), lambda i: (0, i))
    tail = pl.BlockSpec((2, TAIL, wide), lambda i: (0, 0, i))
    slot = pl.BlockSpec((2, count, wide), lambda i: (0, 0, i))
    columns = TAIL + rows + count
    return pl.pallas_call(
        kernel,
        grid=(feats // wide,),
        in_specs=[own, own, own, own, tail, slot],
        out_specs=[own, own, own, own, tail, slot],
        out_shape=[
            jax.ShapeDtypeStruct((rows, feats), jnp.bfloat16),
            jax.ShapeDtypeStruct((rows, feats), jnp.bfloat16),
            jax.ShapeDtypeStruct((rows, feats), jnp.float32),
            jax.ShapeDtypeStruct((rows, feats), jnp.float32),
            jax.ShapeDtypeStruct((2, TAIL, feats), jnp.bfloat16),
            jax.ShapeDtypeStruct((2, count, feats), jnp.bfloat16),
        ],
        scratch_shapes=[pltpu.VMEM((rows, columns), jnp.float32)],
        compiler_params=pltpu.CompilerParams(vmem_limit_bytes=40 * 1024 * 1024),
        cost_estimate=pl.CostEstimate(
            flops=10 * rows * columns * feats,
            bytes_accessed=24 * rows * feats,
            transcendentals=HEADS * rows * columns,
        ),
    )(query_rows, key_rows, value_rows, out_grad, halo, slots)


def body(query_rows, key_rows, value_rows, out_grad):
    rows, feats = query_rows.shape
    shard = lax.axis_index("seq")
    shards = lax.axis_size("seq")
    lead = (shard * rows + OFF) % BLOCK
    halo = shifted(jnp.stack([key_rows[rows - TAIL :], value_rows[rows - TAIL :]]), "seq", 1)
    index = [BLOCK - 1 - lead + BLOCK * i for i in range(SLOT_DEV)]
    own_slots = jnp.stack([
        jnp.concatenate([
            jnp.where(i < rows, lax.dynamic_slice_in_dim(array, jnp.minimum(i, rows - 1), 1, 0), 0)
            for i in index
        ])
        for array in (key_rows, value_rows)
    ])
    slots = lax.all_gather(own_slots, "seq", axis=1, tiled=True)
    attended, query_grad, key_own, value_own, halo_grad, slot_grad = attention(
        query_rows, key_rows, value_rows, out_grad, halo, slots
    )
    after = shifted(halo_grad, "seq", -1)
    parts = lax.all_to_all(
        slot_grad.reshape(2, shards, SLOT_DEV, feats), "seq", split_axis=1, concat_axis=1, tiled=True
    )
    mine = jnp.sum(parts.astype(jnp.float32), axis=1)
    row = jnp.arange(rows, dtype=jnp.int32)[:, None]

    def total(own, i):
        grad = own + jnp.pad(after[i].astype(jnp.float32), ((rows - TAIL, 0), (0, 0)))
        for s in range(SLOT_DEV):
            grad = grad + jnp.where(row == index[s], mine[i, s][None, :], 0.0)
        return grad.astype(jnp.bfloat16)

    return attended, query_grad, total(key_own, 0), total(value_own, 1)


def solution(mesh):
    spec = P(("groups", "seq"), None)
    return jax.shard_map(
        body, mesh=mesh, in_specs=(spec,) * 4, out_specs=(spec,) * 4, check_vma=False
    )
```

time: 185 us -> 77.1 us (0.42)
  waiting for transfers between devices: 46.9 us -> 12.5 us
  local copies, waits for them, and re-layouts: 47 us -> 12.7 us
  other arithmetic: 26.2 us -> 3.23 us
  matrix products: 19.6 us -> 0 us
  between operations: 15.2 us -> 0.77 us
  Pallas kernels: 0 us -> 13.6 us
  starting transfers between devices: 7.15 us -> 10.4 us
    unnamed x2 -> x0, waiting for transfers between devices: 46 us -> none
    dot_general x12 -> x0, matrix products: 19.6 us -> none  [the longest x1 2.93 us: body(): jnp.einsum('hnij,nihd->njhd', local_ds, q_frame, preferred_element_type=j...]
    pallas_call x0 -> x1, Pallas kernels: none -> 13.6 us  [attention(): pl.pallas_call(kernel, grid=(feats // wide,), in_specs=[own, own, own, ow...]
    unnamed x61 -> x14, local copies, waits for them, and re-layouts: 20 us -> 7.42 us
    scatter-add x3 -> x0, other arithmetic: 9.88 us -> none  [the longest x1 3.53 us: body(): key_sum = key_sum.at[clipped].add(jnp.where(live, mine[:, :feats], 0.0))]
    all_to_all x0 -> x1, waiting for transfers between devices: none -> 7.46 us  [body(): lax.all_to_all(slot_grad.reshape(2, shards, SLOT_DEV, feats), 'seq', spli...]
    transpose x3 -> x0, local copies, waits for them, and re-layouts: 7.2 us -> none  [the longest x1 3.61 us: body(): jnp.einsum('hnij,nihd->njhd', local_ds, q_frame, preferred_element_type=j...]
    dynamic_slice x5 -> x0, local copies, waits for them, and re-layouts: 4.98 us -> none  [the longest x4 4.89 us: unframed(): return lax.dynamic_slice_in_dim(whole, lead, rows, 0)]
  transfers between devices with their start and end apart: 3 -> 3, of which waited for: 2 -> 2; matrix products, arithmetic and copies ran while one was open for 24% -> 2% of each run, Pallas kernels for 0% -> 0%
where the time goes in v1:
time: 77.1 us; the launch traced here: 75.6 us
  blocking collectives  22.4 us (29%)
  Pallas kernels  13.6 us (18%)
  local copies, waits for them, and re-layouts  12.7 us (16%)
  waiting for transfers between devices  12.5 us (16%)
  starting transfers between devices  10.4 us (13%)
  other arithmetic  3.23 us (4%)
    all_gather x1, blocking collectives, body(): slots = lax.all_gather(own_slots, 'seq', axis=1, tiled=True)  22.4 us
    pallas_call x1, Pallas kernels, attention(): pl.pallas_call(kernel, grid=(feats // wide,), in_specs=[own, own, own, ow...  13.6 us
    all_to_all x1, waiting for transfers between devices, body(): lax.all_to_all(slot_grad.reshape(2, shards, SLOT_DEV, feats), 'seq', spli...  7.46 us
    unnamed x14, local copies, waits for them, and re-layouts  7.42 us
    ppermute x2, starting transfers between devices, shifted(): return lax.ppermute(block, axis, route)  6.55 us
    ppermute x2, waiting for transfers between devices, shifted(): return lax.ppermute(block, axis, route)  5.03 us
    all_to_all x1, starting transfers between devices, body(): lax.all_to_all(slot_grad.reshape(2, shards, SLOT_DEV, feats), 'seq', spli...  3.86 us
    reshape x2, local copies, waits for them, and re-layouts, body(): slot_grad.reshape(2, shards, SLOT_DEV, feats)  2.8 us
  transfers between devices with their start and end apart: 3, of which 2 were waited for; matrix products, arithmetic and copies ran while one was open for 2% of the time, Pallas kernels for 0%

profile of v1, /device:TPU:1, one launch (start us, length us, event | category | flops | bytes accessed | tf_op | source)
XLA Modules:
  0.0 75.6 jit_solution(12068011628138340229)
XLA Ops:
  0.6 1.2 %slice_bitcast_fusion.2 = (bf16[1,96,2048]{2,1,0:T(8,128)(2,1)S(1)}, bf16[1,96,2048]{2,1,0:T(8,128)(2,1)S(1)}) fusion(bf16[192,2048]{1,0:T(8,128)(2,1)} %v_ref.1, bf16[192,2048]{1,0:T(8,128)(2,1)} %k_ref.1), kind=kLoop, calls=%fused_computation.6 | loop fusion | bytes 1572864 | tf_op jit(solution)/shard_map/stack | solution.py:128
  1.8 0.1 pad_maximum_fusion
  1.9 4.5 %collective-permute-start = (bf16[2,96,2048]{2,1,0:T(8,128)(2,1)S(1)}, bf16[2,96,2048]{2,1,0:T(8,128)(2,1)S(1)}, u32[]{:S(2)}, u32[]{:S(2)}) collective-permute-start(bf16[2,96,2048]{2,1,0:T(8,128)(2,1)S(1)} %pad_maximum_fusion), channel_id=1, source_target_pairs={{0,1},{1,2},{2,3},{3,4},{4,5},{5,6},{6,7},{7,8},{8,9},{9,10},{10,1... | collective-permute-start | bytes 2359304 | tf_op jit(solution)/shard_map/ppermute | solution.py:25
  6.5 0.9 %broadcast_select_fusion.2 = (bf16[1,2048]{1,0:T(2,128)(2,1)S(1)}, bf16[1,2048]{1,0:T(2,128)(2,1)S(1)}, bf16[1,2048]{1,0:T(2,128)(2,1)S(1)}, bf16[1,2048]{1,0:T(2,128)(2,1)S(1)}) fusion(pred[]{:T(512)S(6)} %lt.23, bf16[192,2048]{1,0:T(8,128)(2,1)} %v_ref.1, s32[]{:T(128)S(6)} %select_n.52, s32[]{:T(128)S(6)} %select_n.55, pred[]{:T(512)S(6)} %lt.25, ...), kind=kLoop, calls=%fused_computation.11 | loop fusion | flops 8192 | bytes 32778 | tf_op jit(solution)/shard_map/jit(_where)/select_n | solution.py:132
  7.5 22.4 %all_gather.3 = bf16[2,32,2048]{2,0,1:T(2,128)(2,1)S(1)} all-gather(bf16[2,2,2048]{2,0,1:T(2,128)(2,1)S(1)} %copy.11), channel_id=1, replica_groups=mesh['groups'=2,'seq'=16] {'seq'}, dimensions={1}, use_global_device_ids=true | all-gather | bytes 278528 | tf_op jit(solution)/shard_map/all_gather | solution.py:137
  29.9 0.1 copy.12.slot_ref
  29.9 0.0 collective-permute-done.halo_ref
  30.0 0.0 copy-start.4
  30.0 0.9 %copy-done.4 = bf16[2,96,2048]{2,1,0:T(8,128)(2,1)} copy-done((bf16[2,96,2048]{2,1,0:T(8,128)(2,1)}, bf16[2,96,2048]{2,1,0:T(8,128)(2,1)S(1)}, u32[]{:S(2)}) %copy-start.4) | copy-done | bytes 786456
  30.8 0.0 copy-start
  30.8 1.1 %copy-done = bf16[192,2048]{1,0:T(8,128)(2,1)S(1)} copy-done((bf16[192,2048]{1,0:T(8,128)(2,1)S(1)}, bf16[192,2048]{1,0:T(8,128)(2,1)}, u32[]{:S(2)}) %copy-start) | copy-done | bytes 786456
  32.0 0.0 copy-start.1
  32.0 1.1 %copy-done.1 = bf16[192,2048]{1,0:T(8,128)(2,1)S(1)} copy-done((bf16[192,2048]{1,0:T(8,128)(2,1)S(1)}, bf16[192,2048]{1,0:T(8,128)(2,1)}, u32[]{:S(2)}) %copy-start.1) | copy-done | bytes 786456
  33.1 0.0 copy-start.2
  33.1 1.1 %copy-done.2 = bf16[192,2048]{1,0:T(8,128)(2,1)S(1)} copy-done((bf16[192,2048]{1,0:T(8,128)(2,1)S(1)}, bf16[192,2048]{1,0:T(8,128)(2,1)}, u32[]{:S(2)}) %copy-start.2) | copy-done | bytes 786456
  34.2 0.0 copy-start.3
  34.2 1.1 %copy-done.3 = bf16[192,2048]{1,0:T(8,128)(2,1)S(1)} copy-done((bf16[192,2048]{1,0:T(8,128)(2,1)S(1)}, bf16[192,2048]{1,0:T(8,128)(2,1)}, u32[]{:S(2)}) %copy-start.3) | copy-done | bytes 786456
  35.4 0.0 copy-start.5
  35.4 1.1 %copy-done.5 = bf16[2,96,2048]{2,1,0:T(8,128)(2,1)S(1)} copy-done((bf16[2,96,2048]{2,1,0:T(8,128)(2,1)S(1)}, bf16[2,96,2048]{2,1,0:T(8,128)(2,1)}, u32[]{:S(2)}) %copy-start.5) | copy-done | bytes 786456
  36.5 13.6 %shard_map.75 = (bf16[192,2048]{1,0:T(8,128)(2,1)}, bf16[192,2048]{1,0:T(8,128)(2,1)}, f32[192,2048]{1,0:T(8,128)S(1)}, f32[192,2048]{1,0:T(8,128)S(1)}, bf16[2,...) custom-call(bf16[192,2048]{1,0:T(8,128)(2,1)S(1)} %copy-done.2, bf16[192,2048]{1,0:T(8,128)(2,1)S(1)} %copy-done, ...), custom_call_target="tpu_custom_call" | custom-call | flops 1258291200 | bytes 9437184 | tf_op jit(solution)/shard_map/pallas_call | solution.py:100
  50.1 0.0 copy-start.6
  50.1 0.9 %copy-done.6 = bf16[2,96,2048]{2,1,0:T(8,128)(2,1)} copy-done((bf16[2,96,2048]{2,1,0:T(8,128)(2,1)}, bf16[2,96,2048]{2,1,0:T(8,128)(2,1)S(1)}, u32[]{:S(2)}) %copy-start.6) | copy-done | bytes 786456
  51.0 0.9 %reshape.29 = bf16[2,16,2,2048]{3,2,1,0:T(2,128)(2,1)} reshape(bf16[2,32,2048]{2,1,0:T(8,128)(2,1)S(1)} %get-tuple-element.14) | data formatting | bytes 524288 | tf_op jit(solution)/shard_map/reshape | solution.py:143
  51.9 1.9 %copy.13 = bf16[2,16,2,2048]{3,2,0,1:T(2,128)(2,1)} copy(bf16[2,16,2,2048]{3,2,1,0:T(2,128)(2,1)} %reshape.29) | data formatting | bytes 524288 | tf_op jit(solution)/shard_map/reshape | solution.py:143
  53.8 3.9 %all-to-all-start = ((bf16[2,16,2,2048]{3,2,0,1:T(2,128)(2,1)}), bf16[2,16,2,2048]{3,2,0,1:T(2,128)(2,1)S(1)}, u32[]{:S(2)}, u32[]{:S(2)}) async-start(bf16[2,16,2,2048]{3,2,0,1:T(2,128)(2,1)} %copy.13), calls=%async_computation | async-start | bytes 524288 | tf_op jit(solution)/shard_map/all_to_all | solution.py:142
  57.7 2.0 %collective-permute-start.1 = (bf16[2,96,2048]{2,1,0:T(8,128)(2,1)}, bf16[2,96,2048]{2,1,0:T(8,128)(2,1)}, u32[]{:S(2)}, u32[]{:S(2)}) collective-permute-start(bf16[2,96,2048]{2,1,0:T(8,128)(2,1)} %copy-done.6), channel_id=1, source_target_pairs={{1,0},{2,1},{3,2},{4,3},{5,4},{6,5},{7,6},{8,7},{9,8},{10,9},{11,1... | collective-permute-start | bytes 2359304 | tf_op jit(solution)/shard_map/ppermute | solution.py:25
  59.7 7.5 %all-to-all-done = bf16[2,16,2,2048]{3,2,0,1:T(2,128)(2,1)S(1)} async-done(((bf16[2,16,2,2048]{3,2,0,1:T(2,128)(2,1)}), bf16[2,16,2,2048]{3,2,0,1:T(2,128)(2,1)S(1)}, u32[]{:S(2)}, u32[]{:S(2)}) %all-to-all-start) | async-done | bytes 262176 | tf_op jit(solution)/shard_map/all_to_all | solution.py:142
  67.1 0.2 convert_reduce_fusion
  67.4 5.0 %collective-permute-done.1 = bf16[2,96,2048]{2,1,0:T(8,128)(2,1)} collective-permute-done((bf16[2,96,2048]{2,1,0:T(8,128)(2,1)}, bf16[2,96,2048]{2,1,0:T(8,128)(2,1)}, u32[]{:S(2)}, u32[]{:S(2)}) %collective-permute-start.1) | collective-permute-done | bytes 786464 | tf_op jit(solution)/shard_map/ppermute | solution.py:25
  72.4 1.2 %slice_bitcast_fusion = (bf16[96,2048]{1,0:T(8,128)(2,1)S(1)}, bf16[96,2048]{1,0:T(8,128)(2,1)S(1)}) fusion(bf16[2,96,2048]{2,1,0:T(8,128)(2,1)} %collective-permute-done.1), kind=kLoop, calls=%fused_computation.4 | loop fusion | bytes 1572864 | tf_op jit(solution)/shard_map/convert_element_type | solution.py:149
  73.6 2.0 %add_convert_fusion = (bf16[192,2048]{1,0:T(8,128)(2,1)}, bf16[192,2048]{1,0:T(8,128)(2,1)}) fusion(f32[192,2048]{1,0:T(8,128)S(1)} %get-tuple-element.15, f32[2048]{0:T(1024)S(1)} %bitcast.17, f32[2048]{0:T(1024)S(1)} %bitcast.16, bf16[96,2048]{1,0:T(8,128)(2,1)S(1)} %get-tuple-element.16, pred[192]{0:T(512)(128)(4,1)S(1)} %get-tuple-element.32, ...), kind=kLoop, calls=%fused_computation | loop fusion | flops 5505024 | bytes 5538176 | tf_op jit(solution)/shard_map/convert_element_type | solution.py:152
  (6 shorter events, 0.1 us)
Async XLA Ops:
  1.9 28.0 %collective-permute-start = (bf16[2,96,2048]{2,1,0:T(8,128)(2,1)S(1)}, bf16[2,96,2048]{2,1,0:T(8,128)(2,1)S(1)}, u32[]{:S(2)}, u32[]{:S(2)}) collective-permute-start(bf16[2,96,2048]{2,1,0:T(8,128)(2,1)S(1)} %pad_maximum_fusion), channel_id=1, source_target_pairs={{0,1},{1,2},{2,3},{3,4},{4,5},{5,6},{6,7},{7,8},{8,9},{9,10},{10,1... | collective-permute-start | bytes 2359304 | tf_op jit(solution)/shard_map/ppermute | solution.py:25
  30.0 0.9 %copy-start.4 = (bf16[2,96,2048]{2,1,0:T(8,128)(2,1)}, bf16[2,96,2048]{2,1,0:T(8,128)(2,1)S(1)}, u32[]{:S(2)}) copy-start(bf16[2,96,2048]{2,1,0:T(8,128)(2,1)S(1)} %collective-permute-done.halo_ref) | copy-start | bytes 2359300
  30.8 1.1 %copy-start = (bf16[192,2048]{1,0:T(8,128)(2,1)S(1)}, bf16[192,2048]{1,0:T(8,128)(2,1)}, u32[]{:S(2)}) copy-start(bf16[192,2048]{1,0:T(8,128)(2,1)} %k_ref.1) | copy-start | bytes 2359300
  32.0 1.1 %copy-start.1 = (bf16[192,2048]{1,0:T(8,128)(2,1)S(1)}, bf16[192,2048]{1,0:T(8,128)(2,1)}, u32[]{:S(2)}) copy-start(bf16[192,2048]{1,0:T(8,128)(2,1)} %v_ref.1) | copy-start | bytes 2359300
  33.1 1.1 %copy-start.2 = (bf16[192,2048]{1,0:T(8,128)(2,1)S(1)}, bf16[192,2048]{1,0:T(8,128)(2,1)}, u32[]{:S(2)}) copy-start(bf16[192,2048]{1,0:T(8,128)(2,1)} %q_ref.1) | copy-start | bytes 2359300
  34.2 1.1 %copy-start.3 = (bf16[192,2048]{1,0:T(8,128)(2,1)S(1)}, bf16[192,2048]{1,0:T(8,128)(2,1)}, u32[]{:S(2)}) copy-start(bf16[192,2048]{1,0:T(8,128)(2,1)} %g_ref.1) | copy-start | bytes 2359300
  35.4 1.1 %copy-start.5 = (bf16[2,96,2048]{2,1,0:T(8,128)(2,1)S(1)}, bf16[2,96,2048]{2,1,0:T(8,128)(2,1)}, u32[]{:S(2)}) copy-start(bf16[2,96,2048]{2,1,0:T(8,128)(2,1)} %copy-done.4) | copy-start | bytes 2359300
  50.1 0.9 %copy-start.6 = (bf16[2,96,2048]{2,1,0:T(8,128)(2,1)}, bf16[2,96,2048]{2,1,0:T(8,128)(2,1)S(1)}, u32[]{:S(2)}) copy-start(bf16[2,96,2048]{2,1,0:T(8,128)(2,1)S(1)} %get-tuple-element.13) | copy-start | bytes 2359300
  53.8 13.4 %all-to-all-start = ((bf16[2,16,2,2048]{3,2,0,1:T(2,128)(2,1)}), bf16[2,16,2,2048]{3,2,0,1:T(2,128)(2,1)S(1)}, u32[]{:S(2)}, u32[]{:S(2)}) async-start(bf16[2,16,2,2048]{3,2,0,1:T(2,128)(2,1)} %copy.13), calls=%async_computation | async-start | bytes 524288 | tf_op jit(solution)/shard_map/all_to_all | solution.py:142
  57.7 14.8 %collective-permute-start.1 = (bf16[2,96,2048]{2,1,0:T(8,128)(2,1)}, bf16[2,96,2048]{2,1,0:T(8,128)(2,1)}, u32[]{:S(2)}, u32[]{:S(2)}) collective-permute-start(bf16[2,96,2048]{2,1,0:T(8,128)(2,1)} %copy-done.6), channel_id=1, source_target_pairs={{1,0},{2,1},{3,2},{4,3},{5,4},{6,5},{7,6},{8,7},{9,8},{10,9},{11,1... | collective-permute-start | bytes 2359304 | tf_op jit(solution)/shard_map/ppermute | solution.py:25

commit v2 on v1

v2 whole, which is shorter than its diff:
```python
import functools
import math

import jax
import jax.numpy as jnp
from jax import lax
from jax.experimental import pallas as pl
from jax.experimental.pallas import tpu as pltpu
from jax.sharding import PartitionSpec as P

HEADS = 16
HEAD_DIM = 128
BLOCK = 128
OFF = 32
TAIL = 96
SLOT_DEV = 2
HEADS_STEP = 4
SCALE = 1.0 / math.sqrt(HEAD_DIM)
NEG = -1e30


def bias_of(shard, rows, slots):
    first = shard * rows
    shape = (rows, TAIL + rows)
    query = first + lax.broadcasted_iota(jnp.int32, shape, 0)
    pos = first - TAIL + lax.broadcasted_iota(jnp.int32, shape, 1)
    local = (pos >= 0) & (pos <= query) & ((pos + OFF) >> 7 == (query + OFF) >> 7)
    shape = (rows, slots)
    query = first + lax.broadcasted_iota(jnp.int32, shape, 0)
    slot = lax.broadcasted_iota(jnp.int32, shape, 1)
    start = (slot >> 1) * rows
    offset = BLOCK - 1 - ((start + OFF) & (BLOCK - 1)) + BLOCK * (slot & 1)
    summary = (offset < rows) & ((start + offset + OFF) >> 7 < (query + OFF) >> 7)
    return (
        jnp.where(local, 0.0, NEG).astype(jnp.float32),
        jnp.where(summary, 0.0, NEG).astype(jnp.float32),
    )


def dot(a, b, dims):
    return lax.dot_general(a, b, (dims, ((), ())), preferred_element_type=jnp.float32)


NT = ((1,), (1,))
NN = ((1,), (0,))
TN = ((0,), (0,))


def one_head(q, k, v, g, bias):
    scores = dot(q, k, NT) * SCALE + bias
    top = jnp.max(scores, axis=1, keepdims=True)
    expo = jnp.exp(scores - top)
    prob = expo * (1.0 / jnp.sum(expo, axis=1, keepdims=True))
    weights = prob.astype(jnp.bfloat16)
    attended = dot(weights, v, NN).astype(jnp.bfloat16)
    delta = jnp.sum(g.astype(jnp.float32) * attended.astype(jnp.float32), axis=1, keepdims=True)
    dscores = (prob * (dot(g, v, NT) - delta)).astype(jnp.bfloat16)
    qgrad = (dot(dscores, k, NN) * SCALE).astype(jnp.bfloat16)
    return attended, qgrad, dot(dscores, q, TN) * SCALE, dot(weights, g, TN)


def remote(src, dst, send, recv, seq):
    return pltpu.make_async_remote_copy(
        src_ref=src, dst_ref=dst, send_sem=send, recv_sem=recv,
        device_id={"seq": seq}, device_id_type=pl.DeviceIdType.MESH,
    )


def kernel(shards, q_ref, k_ref, v_ref, g_ref, mine_ref, out_ref, qg_ref, kg_ref, vg_ref, after_ref,
           sum_ref, bias_ref, halo_ref, hg_ref, slot_ref, part_ref, got_ref, ks_ref, vs_ref,
           kp_ref, vp_ref, halo_send, halo_recv, slot_send, slot_recv, back_send, back_recv,
           part_send, part_recv):
    rows, feats = q_ref.shape
    slots = shards * SLOT_DEV
    half = SLOT_DEV * HEADS
    wide = HEADS_STEP * HEAD_DIM
    steps = feats // wide
    me = lax.axis_index("seq")
    last = shards - 1
    prior, following = jnp.maximum(me - 1, 0), jnp.minimum(me + 1, last)
    lead = lax.rem(me * rows + OFF, BLOCK)
    lead_next = lax.rem((me + 1) * rows + OFF, BLOCK)
    ways = ((TAIL, lambda x: x > OFF), (OFF, lambda x: x <= OFF))

    slot_ref[...] = jnp.zeros_like(slot_ref)
    got_ref[...] = jnp.zeros_like(got_ref)
    halo_ref[...] = jnp.zeros_like(halo_ref)
    after_ref[...] = jnp.zeros_like(after_ref)
    slot_ref[me] = mine_ref[...]

    barrier = pltpu.get_barrier_semaphore()

    def greet(p, carry):
        @pl.when(p != me)
        def _():
            pl.semaphore_signal(
                barrier, inc=1, device_id={"seq": p}, device_id_type=pl.DeviceIdType.MESH
            )
        return carry

    lax.fori_loop(0, shards, greet, 0)
    pl.semaphore_wait(barrier, shards - 1)

    def halo_copy(i, size):
        return remote(
            (k_ref, v_ref)[i].at[pl.ds(rows - size, size)],
            halo_ref.at[i, pl.ds(TAIL - size, size)],
            halo_send.at[i], halo_recv.at[i], following,
        )

    def back_copy(j, size):
        part = (slice(None), pl.ds(TAIL - size, size), pl.ds(pl.multiple_of(j * wide, wide), wide))
        return remote(
            hg_ref.at[part], after_ref.at[part], back_send.at[j], back_recv.at[j], prior
        )

    def slot_copy(p, owner):
        return remote(mine_ref, slot_ref.at[owner], slot_send.at[p], slot_recv.at[owner], p)

    def part_copy(p, sender):
        return remote(part_ref.at[p], got_ref.at[sender], part_send.at[p], part_recv.at[sender], p)

    def each(low, high, action):
        def step(p, carry):
            action(p)
            return carry
        lax.fori_loop(low, high, step, 0)

    for size, fits in ways:
        @pl.when((me < last) & fits(lead_next))
        def _():
            for i in range(2):
                halo_copy(i, size).start()
    each(me + 1, shards, lambda p: slot_copy(p, me).start())

    local, summary = bias_of(me, rows, slots)
    bias_ref[:, : TAIL + rows] = local
    bias_ref[:, TAIL + rows :] = summary

    for size, fits in ways:
        @pl.when((me > 0) & fits(lead))
        def _():
            for i in range(2):
                halo_copy(i, size).wait_recv()
    each(0, me, lambda p: slot_copy(p, p).wait_recv())

    ks_ref[...] = slot_ref[:, :half].astype(jnp.float32).reshape(shards * half, HEAD_DIM)
    vs_ref[...] = slot_ref[:, half:].astype(jnp.float32).reshape(shards * half, HEAD_DIM)

    def group(j, carry):
        for i in range(HEADS_STEP):
            h = j * HEADS_STEP + i
            c = pl.ds(pl.multiple_of(h * HEAD_DIM, HEAD_DIM), HEAD_DIM)
            of_head = pl.ds(h, slots, stride=HEADS)
            k_slots = ks_ref[of_head, :].astype(jnp.bfloat16)
            v_slots = vs_ref[of_head, :].astype(jnp.bfloat16)
            k = jnp.concatenate([halo_ref[0, :, c], k_ref[:, c], k_slots], axis=0)
            v = jnp.concatenate([halo_ref[1, :, c], v_ref[:, c], v_slots], axis=0)
            attended, qgrad, kg, vg = one_head(q_ref[:, c], k, v, g_ref[:, c], bias_ref[...])
            out_ref[:, c] = attended
            qg_ref[:, c] = qgrad
            for n, (grad, own_ref, term_ref) in enumerate(((kg, kg_ref, kp_ref), (vg, vg_ref, vp_ref))):
                hg_ref[n, :, c] = grad[:TAIL].astype(jnp.bfloat16)
                own_ref[:, c] = grad[TAIL : TAIL + rows]
                term_ref[of_head, :] = grad[TAIL + rows :]
        for size, fits in ways:
            @pl.when((me > 0) & fits(lead))
            def _():
                back_copy(j, size).start()
        return carry

    lax.fori_loop(0, steps, group, 0)

    part_ref[:, :half] = kp_ref[...].astype(jnp.bfloat16).reshape(shards, half, HEAD_DIM)
    part_ref[:, half:] = vp_ref[...].astype(jnp.bfloat16).reshape(shards, half, HEAD_DIM)
    each(0, me, lambda p: part_copy(p, me).start())
    got_ref[me] = part_ref[me]
    for size, fits in ways:
        @pl.when((me < last) & fits(lead_next))
        def _():
            each(0, steps, lambda j: back_copy(j, size).wait_recv())
    each(me + 1, shards, lambda p: part_copy(p, p).wait_recv())
    sum_ref[...] = jnp.sum(got_ref[...].astype(jnp.float32), axis=0)

    for size, fits in ways:
        @pl.when((me < last) & fits(lead_next))
        def _():
            for i in range(2):
                halo_copy(i, size).wait_send()

        @pl.when((me > 0) & fits(lead))
        def _():
            each(0, steps, lambda j: back_copy(j, size).wait_send())
    each(me + 1, shards, lambda p: slot_copy(p, me).wait_send())
    each(0, me, lambda p: part_copy(p, me).wait_send())


def attention(query_rows, key_rows, value_rows, out_grad, own_slots):
    rows, feats = query_rows.shape
    shards = lax.axis_size("seq")
    slots = shards * SLOT_DEV
    half = SLOT_DEV * HEADS
    columns = TAIL + rows + slots
    steps = feats // (HEADS_STEP * HEAD_DIM)
    vmem = pl.BlockSpec(memory_space=pltpu.VMEM)
    bf16, f32 = jnp.bfloat16, jnp.float32
    return pl.pallas_call(
        functools.partial(kernel, shards),
        in_specs=[vmem] * 5,
        out_specs=[vmem] * 6,
        out_shape=[
            jax.ShapeDtypeStruct((rows, feats), bf16),
            jax.ShapeDtypeStruct((rows, feats), bf16),
            jax.ShapeDtypeStruct((rows, feats), f32),
            jax.ShapeDtypeStruct((rows, feats), f32),
            jax.ShapeDtypeStruct((2, TAIL, feats), bf16),
            jax.ShapeDtypeStruct((2 * half, HEAD_DIM), f32),
        ],
        scratch_shapes=[
            pltpu.VMEM((rows, columns), f32),
            pltpu.VMEM((2, TAIL, feats), bf16),
            pltpu.VMEM((2, TAIL, feats), bf16),
            pltpu.VMEM((shards, 2 * half, HEAD_DIM), bf16),
            pltpu.VMEM((shards, 2 * half, HEAD_DIM), bf16),
            pltpu.VMEM((shards, 2 * half, HEAD_DIM), bf16),
            pltpu.VMEM((shards * half, HEAD_DIM), f32),
            pltpu.VMEM((shards * half, HEAD_DIM), f32),
            pltpu.VMEM((shards * half, HEAD_DIM), f32),
            pltpu.VMEM((shards * half, HEAD_DIM), f32),
            pltpu.SemaphoreType.DMA((2,)),
            pltpu.SemaphoreType.DMA((2,)),
            pltpu.SemaphoreType.DMA((shards,)),
            pltpu.SemaphoreType.DMA((shards,)),
            pltpu.SemaphoreType.DMA((steps,)),
            pltpu.SemaphoreType.DMA((steps,)),
            pltpu.SemaphoreType.DMA((shards,)),
            pltpu.SemaphoreType.DMA((shards,)),
        ],
        compiler_params=pltpu.CompilerParams(
            vmem_limit_bytes=48 * 1024 * 1024, collective_id=0, has_side_effects=True
        ),
        cost_estimate=pl.CostEstimate(
            flops=10 * rows * columns * feats,
            bytes_accessed=24 * rows * feats,
            transcendentals=HEADS * rows * columns,
        ),
    )(query_rows, key_rows, value_rows, out_grad, own_slots)


def body(query_rows, key_rows, value_rows, out_grad):
    rows, feats = query_rows.shape
    shard = lax.axis_index("seq")
    lead = (shard * rows + OFF) % BLOCK
    index = [BLOCK - 1 - lead + BLOCK * i for i in range(SLOT_DEV)]
    own_slots = jnp.stack([
        jnp.concatenate([
            jnp.where(i < rows, lax.dynamic_slice_in_dim(array, jnp.minimum(i, rows - 1), 1, 0), 0)
            for i in index
        ])
        for array in (key_rows, value_rows)
    ])
    attended, query_grad, key_own, value_own, after, terms = attention(
        query_rows, key_rows, value_rows, out_grad, own_slots.reshape(-1, HEAD_DIM)
    )
    mine = terms.reshape(2, SLOT_DEV, feats)
    row = jnp.arange(rows, dtype=jnp.int32)[:, None]

    def total(own, i):
        grad = own + jnp.pad(after[i].astype(jnp.float32), ((rows - TAIL, 0), (0, 0)))
        for s in range(SLOT_DEV):
            grad = grad + jnp.where(row == index[s], mine[i, s][None, :], 0.0)
        return grad.astype(jnp.bfloat16)

    return attended, query_grad, total(key_own, 0), total(value_own, 1)


def solution(mesh):
    spec = P(("groups", "seq"), None)
    return jax.shard_map(
        body, mesh=mesh, in_specs=(spec,) * 4, out_specs=(spec,) * 4, check_vma=False
    )
```

time: 77.1 us -> 49.1 us (0.64); the launches traced: 75.6 us -> 48.4 us
  blocking collectives: 22.4 us -> 0 us
  Pallas kernels: 13.6 us -> 35.6 us
  waiting for transfers between devices: 12.5 us -> 0 us
  starting transfers between devices: 10.4 us -> 0 us
  local copies, waits for them, and re-layouts: 12.7 us -> 7.71 us
  other arithmetic: 3.23 us -> 4.35 us
    all_gather x1 -> x0, blocking collectives: 22.4 us -> none  [body(): slots = lax.all_gather(own_slots, 'seq', axis=1, tiled=True)]
    pallas_call x1, Pallas kernels: 13.6 us -> 35.6 us  [attention(): pl.pallas_call(functools.partial(kernel, shards), in_specs=[vmem] * 5, ou...]
    all_to_all x1 -> x0, waiting for transfers between devices: 7.46 us -> none  [body(): lax.all_to_all(slot_grad.reshape(2, shards, SLOT_DEV, feats), 'seq', spli...]
    ppermute x2 -> x0, starting transfers between devices: 6.55 us -> none  [shifted(): return lax.ppermute(block, axis, route)]
    ppermute x2 -> x0, waiting for transfers between devices: 5.03 us -> none  [shifted(): return lax.ppermute(block, axis, route)]
    all_to_all x1 -> x0, starting transfers between devices: 3.86 us -> none  [body(): lax.all_to_all(slot_grad.reshape(2, shards, SLOT_DEV, feats), 'seq', spli...]
    reshape x2, local copies, waits for them, and re-layouts: 2.8 us -> 0.04 us  [the longest x1 0.02 us: body(): mine = terms.reshape(2, SLOT_DEV, feats)]
    convert_element_type x1, other arithmetic: 1.99 us -> 3.4 us  [total(): return grad.astype(jnp.bfloat16)]
  transfers between devices with their start and end apart: 3 -> 0, of which waited for: 2 -> 0; matrix products, arithmetic and copies ran while one was open for 2% -> 0% of each run, Pallas kernels for 0% -> 0%
where the time goes in v2:
time: 49.1 us; the launch traced here: 48.4 us
  Pallas kernels  35.6 us (73%)
  local copies, waits for them, and re-layouts  7.71 us (16%)
  other arithmetic  4.35 us (9%)
  between operations  0.74 us (2%)
    pallas_call x1, Pallas kernels, attention(): pl.pallas_call(functools.partial(kernel, shards), in_specs=[vmem] * 5, ou...  35.6 us
    unnamed x12, local copies, waits for them, and re-layouts  7.59 us
    convert_element_type x1, other arithmetic, total(): return grad.astype(jnp.bfloat16)  3.4 us

profile of v2, /device:TPU:1, one launch (start us, length us, event | category | flops | bytes accessed | tf_op | source)
XLA Modules:
  0.0 48.4 jit_solution(10516989715559349220)
XLA Ops:
  0.7 0.9 %broadcast_select_fusion.2 = (bf16[1,2048]{1,0:T(2,128)(2,1)S(1)}, bf16[1,2048]{1,0:T(2,128)(2,1)S(1)}, bf16[1,2048]{1,0:T(2,128)(2,1)S(1)}, bf16[1,2048]{1,0:T(2,128)(2,1)S(1)}) fusion(pred[]{:T(512)S(6)} %lt.23, bf16[192,2048]{1,0:T(8,128)(2,1)} %v_ref.1, s32[]{:T(128)S(6)} %select_n.52, s32[]{:T(128)S(6)} %select_n.55, pred[]{:T(512)S(6)} %lt.25, ...), kind=kLoop, calls=%fused_computation.7 | loop fusion | flops 8192 | bytes 32778 | tf_op jit(solution)/shard_map/jit(_where)/select_n | solution.py:257
  1.7 0.0 copy-start
  1.7 1.1 %copy-done = bf16[192,2048]{1,0:T(8,128)(2,1)S(1)} copy-done((bf16[192,2048]{1,0:T(8,128)(2,1)S(1)}, bf16[192,2048]{1,0:T(8,128)(2,1)}, u32[]{:S(2)}) %copy-start) | copy-done | bytes 786456
  2.8 0.0 copy-start.1
  2.8 1.1 %copy-done.1 = bf16[192,2048]{1,0:T(8,128)(2,1)S(1)} copy-done((bf16[192,2048]{1,0:T(8,128)(2,1)S(1)}, bf16[192,2048]{1,0:T(8,128)(2,1)}, u32[]{:S(2)}) %copy-start.1) | copy-done | bytes 786456
  3.9 0.0 copy-start.2
  3.9 1.1 %copy-done.2 = bf16[192,2048]{1,0:T(8,128)(2,1)S(1)} copy-done((bf16[192,2048]{1,0:T(8,128)(2,1)S(1)}, bf16[192,2048]{1,0:T(8,128)(2,1)}, u32[]{:S(2)}) %copy-start.2) | copy-done | bytes 786456
  5.1 0.0 copy-start.3
  5.1 1.1 %copy-done.3 = bf16[192,2048]{1,0:T(8,128)(2,1)S(1)} copy-done((bf16[192,2048]{1,0:T(8,128)(2,1)S(1)}, bf16[192,2048]{1,0:T(8,128)(2,1)}, u32[]{:S(2)}) %copy-start.3) | copy-done | bytes 786456
  6.2 35.6 %shard_map.75 = (bf16[192,2048]{1,0:T(8,128)(2,1)S(1)}, bf16[192,2048]{1,0:T(8,128)(2,1)S(1)}, f32[192,2048]{1,0:T(8,128)}, f32[192,2048]{1,0:T(8,128)}, bf16[2,...) custom-call(bf16[192,2048]{1,0:T(8,128)(2,1)S(1)} %copy-done.2, bf16[192,2048]{1,0:T(8,128)(2,1)S(1)} %copy-done, ...), custom_call_target="tpu_custom_call" | custom-call | flops 1258291200 | bytes 9437184 | tf_op jit(solution)/shard_map/pallas_call | solution.py:207
  41.8 0.0 copy-start.4
  41.9 0.1 slice_bitcast_fusion
  41.9 1.3 %copy-done.4 = f32[192,2048]{1,0:T(8,128)S(1)} copy-done((f32[192,2048]{1,0:T(8,128)S(1)}, f32[192,2048]{1,0:T(8,128)}, u32[]{:S(2)}) %copy-start.4) | copy-done | bytes 1572888
  43.2 3.4 %add_convert_fusion = (bf16[192,2048]{1,0:T(8,128)(2,1)}, bf16[192,2048]{1,0:T(8,128)(2,1)}) fusion(f32[192,2048]{1,0:T(8,128)} %get-tuple-element.15, f32[2048]{0:T(1024)S(1)} %bitcast.13, f32[2048]{0:T(1024)S(1)} %bitcast.12, bf16[96,2048]{1,0:T(8,128)(2,1)S(1)} %get-tuple-element.16, pred[192]{0:T(512)(128)(4,1)S(1)} %get-tuple-element.30, ...), kind=kLoop, calls=%fused_computation | loop fusion | flops 5505024 | bytes 5538176 | tf_op jit(solution)/shard_map/convert_element_type | solution.py:272
  46.6 0.9 %copy.10 = bf16[192,2048]{1,0:T(8,128)(2,1)} copy(bf16[192,2048]{1,0:T(8,128)(2,1)S(1)} %get-tuple-element.36) | data formatting | bytes 1572864
  47.5 0.9 %copy.11 = bf16[192,2048]{1,0:T(8,128)(2,1)} copy(bf16[192,2048]{1,0:T(8,128)(2,1)S(1)} %get-tuple-element.37) | data formatting | bytes 1572864
  (7 shorter events, 0.2 us)
Async XLA Ops:
  1.7 1.1 %copy-start = (bf16[192,2048]{1,0:T(8,128)(2,1)S(1)}, bf16[192,2048]{1,0:T(8,128)(2,1)}, u32[]{:S(2)}) copy-start(bf16[192,2048]{1,0:T(8,128)(2,1)} %k_ref.1) | copy-start | bytes 2359300
  2.8 1.1 %copy-start.1 = (bf16[192,2048]{1,0:T(8,128)(2,1)S(1)}, bf16[192,2048]{1,0:T(8,128)(2,1)}, u32[]{:S(2)}) copy-start(bf16[192,2048]{1,0:T(8,128)(2,1)} %v_ref.1) | copy-start | bytes 2359300
  3.9 1.1 %copy-start.2 = (bf16[192,2048]{1,0:T(8,128)(2,1)S(1)}, bf16[192,2048]{1,0:T(8,128)(2,1)}, u32[]{:S(2)}) copy-start(bf16[192,2048]{1,0:T(8,128)(2,1)} %q_ref.1) | copy-start | bytes 2359300
  5.1 1.1 %copy-start.3 = (bf16[192,2048]{1,0:T(8,128)(2,1)S(1)}, bf16[192,2048]{1,0:T(8,128)(2,1)}, u32[]{:S(2)}) copy-start(bf16[192,2048]{1,0:T(8,128)(2,1)} %g_ref.1) | copy-start | bytes 2359300
  41.8 1.4 %copy-start.4 = (f32[192,2048]{1,0:T(8,128)S(1)}, f32[192,2048]{1,0:T(8,128)}, u32[]{:S(2)}) copy-start(f32[192,2048]{1,0:T(8,128)} %get-tuple-element.12) | copy-start | bytes 4718596

commit v3 on v2

--- a/solution.py
+++ b/solution.py
@@ -66,10 +66,10 @@
     )
 
 
-def kernel(shards, q_ref, k_ref, v_ref, g_ref, mine_ref, out_ref, qg_ref, kg_ref, vg_ref, after_ref,
-           sum_ref, bias_ref, halo_ref, hg_ref, slot_ref, part_ref, got_ref, ks_ref, vs_ref,
+def kernel(shards, q_in, k_in, v_in, g_in, mine_ref, out_ref, qg_ref, key_ref, value_ref,
+           q_ref, k_ref, v_ref, g_ref, kg_ref, vg_ref, after_ref, sum_ref, bias_ref, halo_ref, hg_ref, slot_ref, part_ref, got_ref, ks_ref, vs_ref,
            kp_ref, vp_ref, halo_send, halo_recv, slot_send, slot_recv, back_send, back_recv,
-           part_send, part_recv):
+           part_send, part_recv, load_sem):
     rows, feats = q_ref.shape
     slots = shards * SLOT_DEV
     half = SLOT_DEV * HEADS
@@ -82,10 +82,27 @@
     lead_next = lax.rem((me + 1) * rows + OFF, BLOCK)
     ways = ((TAIL, lambda x: x > OFF), (OFF, lambda x: x <= OFF))
 
+    loads = [
+        pltpu.make_async_copy(source, target, load_sem.at[i])
+        for i, (source, target) in enumerate(
+            ((q_in, q_ref), (k_in, k_ref), (v_in, v_ref), (g_in, g_ref))
+        )
+    ]
+    for load in loads:
+        load.start()
+
     slot_ref[...] = jnp.zeros_like(slot_ref)
     got_ref[...] = jnp.zeros_like(got_ref)
-    halo_ref[...] = jnp.zeros_like(halo_ref)
-    after_ref[...] = jnp.zeros_like(after_ref)
+    short = jnp.zeros((2, TAIL - OFF, feats), jnp.bfloat16)
+    rest = jnp.zeros((2, OFF, feats), jnp.bfloat16)
+    for ref, missing, alone in ((halo_ref, lead <= OFF, me == 0), (after_ref, lead_next <= OFF, me == last)):
+        @pl.when(missing | alone)
+        def _():
+            ref[:, : TAIL - OFF] = short
+
+        @pl.when(alone)
+        def _():
+            ref[:, TAIL - OFF :] = rest
     slot_ref[me] = mine_ref[...]
 
     barrier = pltpu.get_barrier_semaphore()
@@ -101,11 +118,12 @@
     lax.fori_loop(0, shards, greet, 0)
     pl.semaphore_wait(barrier, shards - 1)
 
-    def halo_copy(i, size):
+    def halo_copy(i, j, size):
+        cols = pl.ds(pl.multiple_of(j * wide, wide), wide)
         return remote(
-            (k_ref, v_ref)[i].at[pl.ds(rows - size, size)],
-            halo_ref.at[i, pl.ds(TAIL - size, size)],
-            halo_send.at[i], halo_recv.at[i], following,
+            (k_in, v_in)[i].at[pl.ds(rows - size, size), cols],
+            halo_ref.at[i, pl.ds(TAIL - size, size), cols],
+            halo_send.at[i, j], halo_recv.at[i, j], following,
         )
 
     def back_copy(j, size):
@@ -126,28 +144,33 @@
             return carry
         lax.fori_loop(low, high, step, 0)
 
+    each(me + 1, shards, lambda p: slot_copy(p, me).start())
     for size, fits in ways:
         @pl.when((me < last) & fits(lead_next))
         def _():
-            for i in range(2):
-                halo_copy(i, size).start()
-    each(me + 1, shards, lambda p: slot_copy(p, me).start())
+            def send(j):
+                for i in range(2):
+                    halo_copy(i, j, size).start()
+            each(0, steps, send)
 
     local, summary = bias_of(me, rows, slots)
     bias_ref[:, : TAIL + rows] = local
     bias_ref[:, TAIL + rows :] = summary
 
-    for size, fits in ways:
-        @pl.when((me > 0) & fits(lead))
-        def _():
-            for i in range(2):
-                halo_copy(i, size).wait_recv()
     each(0, me, lambda p: slot_copy(p, p).wait_recv())
 
     ks_ref[...] = slot_ref[:, :half].astype(jnp.float32).reshape(shards * half, HEAD_DIM)
     vs_ref[...] = slot_ref[:, half:].astype(jnp.float32).reshape(shards * half, HEAD_DIM)
 
+    for load in loads:
+        load.wait()
+
     def group(j, carry):
+        for size, fits in ways:
+            @pl.when((me > 0) & fits(lead))
+            def _():
+                for i in range(2):
+                    halo_copy(i, j, size).wait_recv()
         for i in range(HEADS_STEP):
             h = j * HEADS_STEP + i
             c = pl.ds(pl.multiple_of(h * HEAD_DIM, HEAD_DIM), HEAD_DIM)
@@ -179,14 +202,33 @@
         @pl.when((me < last) & fits(lead_next))
         def _():
             each(0, steps, lambda j: back_copy(j, size).wait_recv())
+    grads = ((kg_ref, key_ref), (vg_ref, value_ref))
+    for n, (own_ref, _) in enumerate(grads):
+        own_ref[rows - TAIL :] += after_ref[n].astype(jnp.float32)
     each(me + 1, shards, lambda p: part_copy(p, p).wait_recv())
     sum_ref[...] = jnp.sum(got_ref[...].astype(jnp.float32), axis=0)
+    for t in range(SLOT_DEV):
+        index = BLOCK - 1 - lead + BLOCK * t
+
+        @pl.when(index < rows)
+        def _():
+            at = pl.ds(pl.multiple_of(jnp.minimum(index, rows - 1) - 7, 8), 8)
+            ends = lax.broadcasted_iota(jnp.int32, (8, HEAD_DIM), 0) == 7
+            for n, (own_ref, _) in enumerate(grads):
+                for h in range(HEADS):
+                    c = slice(h * HEAD_DIM, (h + 1) * HEAD_DIM)
+                    r = (n * SLOT_DEV + t) * HEADS + h
+                    own_ref[at, c] += jnp.where(ends, sum_ref[r : r + 1, :], 0.0)
+    for own_ref, final_ref in grads:
+        final_ref[...] = own_ref[...].astype(jnp.bfloat16)
 
     for size, fits in ways:
         @pl.when((me < last) & fits(lead_next))
         def _():
-            for i in range(2):
-                halo_copy(i, size).wait_send()
+            def sent(j):
+                for i in range(2):
+                    halo_copy(i, j, size).wait_send()
+            each(0, steps, sent)
 
         @pl.when((me > 0) & fits(lead))
         def _():
@@ -206,17 +248,18 @@
     bf16, f32 = jnp.bfloat16, jnp.float32
     return pl.pallas_call(
         functools.partial(kernel, shards),
-        in_specs=[vmem] * 5,
-        out_specs=[vmem] * 6,
-        out_shape=[
-            jax.ShapeDtypeStruct((rows, feats), bf16),
-            jax.ShapeDtypeStruct((rows, feats), bf16),
-            jax.ShapeDtypeStruct((rows, feats), f32),
-            jax.ShapeDtypeStruct((rows, feats), f32),
-            jax.ShapeDtypeStruct((2, TAIL, feats), bf16),
-            jax.ShapeDtypeStruct((2 * half, HEAD_DIM), f32),
-        ],
+        in_specs=[pl.BlockSpec(memory_space=pl.ANY)] * 4 + [vmem],
+        out_specs=[vmem] * 4,
+        out_shape=[jax.ShapeDtypeStruct((rows, feats), bf16)] * 4,
         scratch_shapes=[
+            pltpu.VMEM((rows, feats), bf16),
+            pltpu.VMEM((rows, feats), bf16),
+            pltpu.VMEM((rows, feats), bf16),
+            pltpu.VMEM((rows, feats), bf16),
+            pltpu.VMEM((rows, feats), f32),
+            pltpu.VMEM((rows, feats), f32),
+            pltpu.VMEM((2, TAIL, feats), bf16),
+            pltpu.VMEM((2 * half, HEAD_DIM), f32),
             pltpu.VMEM((rows, columns), f32),
             pltpu.VMEM((2, TAIL, feats), bf16),
             pltpu.VMEM((2, TAIL, feats), bf16),
@@ -227,17 +270,18 @@
             pltpu.VMEM((shards * half, HEAD_DIM), f32),
             pltpu.VMEM((shards * half, HEAD_DIM), f32),
             pltpu.VMEM((shards * half, HEAD_DIM), f32),
-            pltpu.SemaphoreType.DMA((2,)),
-            pltpu.SemaphoreType.DMA((2,)),
+            pltpu.SemaphoreType.DMA((2, steps)),
+            pltpu.SemaphoreType.DMA((2, steps)),
             pltpu.SemaphoreType.DMA((shards,)),
             pltpu.SemaphoreType.DMA((shards,)),
             pltpu.SemaphoreType.DMA((steps,)),
             pltpu.SemaphoreType.DMA((steps,)),
             pltpu.SemaphoreType.DMA((shards,)),
             pltpu.SemaphoreType.DMA((shards,)),
+            pltpu.SemaphoreType.DMA((4,)),
         ],
         compiler_params=pltpu.CompilerParams(
-            vmem_limit_bytes=48 * 1024 * 1024, collective_id=0, has_side_effects=True
+            vmem_limit_bytes=56 * 1024 * 1024, collective_id=0, has_side_effects=True
         ),
         cost_estimate=pl.CostEstimate(
             flops=10 * rows * columns * feats,
@@ -259,19 +303,9 @@
         ])
         for array in (key_rows, value_rows)
     ])
-    attended, query_grad, key_own, value_own, after, terms = attention(
-        query_rows, key_rows, value_rows, out_grad, own_slots.reshape(-1, HEAD_DIM)
+    return tuple(
+        attention(query_rows, key_rows, value_rows, out_grad, own_slots.reshape(-1, HEAD_DIM))
     )
-    mine = terms.reshape(2, SLOT_DEV, feats)
-    row = jnp.arange(rows, dtype=jnp.int32)[:, None]
-
-    def total(own, i):
-        grad = own + jnp.pad(after[i].astype(jnp.float32), ((rows - TAIL, 0), (0, 0)))
-        for s in range(SLOT_DEV):
-            grad = grad + jnp.where(row == index[s], mine[i, s][None, :], 0.0)
-        return grad.astype(jnp.bfloat16)
-
-    return attended, query_grad, total(key_own, 0), total(value_own, 1)
 
 
 def solution(mesh):

time: 49.1 us -> 45 us (0.916)
  other arithmetic: 4.35 us -> 0.94 us
  local copies, waits for them, and re-layouts: 7.71 us -> 6.5 us
  Pallas kernels: 35.6 us -> 36.2 us
    convert_element_type x1 -> x0, other arithmetic: 3.4 us -> none  [total(): return grad.astype(jnp.bfloat16)]
    unnamed x12 -> x10, local copies, waits for them, and re-layouts: 7.59 us -> 5.88 us
    reshape x1, local copies, waits for them, and re-layouts: 0.02 us -> 0.62 us  [body(): own_slots.reshape(-1, HEAD_DIM)]
    pallas_call x1, Pallas kernels: 35.6 us -> 36.2 us  [attention(): pl.pallas_call(functools.partial(kernel, shards), in_specs=[pl.BlockSpec(...]
where the time goes in v3:
time: 45 us; the launch traced here: 44.3 us
  Pallas kernels  36.2 us (80%)
  local copies, waits for them, and re-layouts  6.5 us (14%)
  other arithmetic  0.94 us (2%)
  between operations  0.7 us (2%)
    pallas_call x1, Pallas kernels, attention(): pl.pallas_call(functools.partial(kernel, shards), in_specs=[pl.BlockSpec(...  36.2 us
    unnamed x10, local copies, waits for them, and re-layouts  5.88 us

profile of v3, /device:TPU:1, one launch (start us, length us, event | category | flops | bytes accessed | tf_op | source)
XLA Modules:
  0.0 44.3 jit_solution(7833419970337672791)
XLA Ops:
  0.7 0.9 %broadcast_select_fusion.2 = (bf16[1,2048]{1,0:T(2,128)(2,1)S(1)}, bf16[1,2048]{1,0:T(2,128)(2,1)S(1)}, bf16[1,2048]{1,0:T(2,128)(2,1)S(1)}, bf16[1,2048]{1,0:T(2,128)(2,1)S(1)}) fusion(pred[]{:T(512)S(6)} %lt.23, bf16[192,2048]{1,0:T(8,128)(2,1)} %v_in.1, s32[]{:T(128)S(6)} %select_n.39, s32[]{:T(128)S(6)} %select_n.42, pred[]{:T(512)S(6)} %lt.25, ...), kind=kLoop, calls=%fused_computation.3 | loop fusion | flops 8192 | bytes 32778 | tf_op jit(solution)/shard_map/jit(_where)/select_n | solution.py:301
  1.6 0.6 %reshape.11.mine_ref = bf16[64,128]{1,0:T(8,128)(2,1)} reshape(bf16[2,2,2048]{2,1,0:T(2,128)(2,1)S(1)} %pad_maximum_fusion) | data formatting | bytes 32768 | tf_op jit(solution)/shard_map/reshape | solution.py:307
  2.2 36.2 %shard_map.75 = (bf16[192,2048]{1,0:T(8,128)(2,1)}, bf16[192,2048]{1,0:T(8,128)(2,1)}, bf16[192,2048]{1,0:T(8,128)(2,1)}, bf16[192,2048]{1,0:T(8,128)(2,1)}) custom-call(bf16[192,2048]{1,0:T(8,128)(2,1)} %q_in.1, bf16[192,2048]{1,0:T(8,128)(2,1)} %k_in.1, bf16[192,2048]{1,0:T(8,128)(2,1)} %v_in.1, bf16[192,2048]{1,0:T(8,128)(2,1)} %g_in.1, ...), custom_call_target="tpu_custom_call" | custom-call | flops 1258291200 | bytes 9437184 | tf_op jit(solution)/shard_map/pallas_call | solution.py:249
  38.4 0.0 copy-start.2
  38.4 2.2 %copy.12 = bf16[192,2048]{1,0:T(8,128)(2,1)} copy(bf16[192,2048]{1,0:T(8,128)(2,1)} %get-tuple-element.14) | data formatting | bytes 1572864
  40.6 0.0 copy-done.2
  40.6 0.0 copy-start.1
  40.6 0.9 %copy.13 = bf16[192,2048]{1,0:T(8,128)(2,1)} copy(bf16[192,2048]{1,0:T(8,128)(2,1)S(1)} %copy-done.2) | data formatting | bytes 1572864
  41.5 0.5 %copy-done.1 = bf16[192,2048]{1,0:T(8,128)(2,1)S(1)} copy-done((bf16[192,2048]{1,0:T(8,128)(2,1)S(1)}, bf16[192,2048]{1,0:T(8,128)(2,1)}, u32[]{:S(2)}) %copy-start.1) | copy-done | bytes 786456
  42.0 0.0 copy-start
  42.0 0.9 %copy.14 = bf16[192,2048]{1,0:T(8,128)(2,1)} copy(bf16[192,2048]{1,0:T(8,128)(2,1)S(1)} %copy-done.1) | data formatting | bytes 1572864
  42.9 0.5 %copy-done = bf16[192,2048]{1,0:T(8,128)(2,1)S(1)} copy-done((bf16[192,2048]{1,0:T(8,128)(2,1)S(1)}, bf16[192,2048]{1,0:T(8,128)(2,1)}, u32[]{:S(2)}) %copy-start) | copy-done | bytes 786456
  43.4 0.9 %copy.15 = bf16[192,2048]{1,0:T(8,128)(2,1)} copy(bf16[192,2048]{1,0:T(8,128)(2,1)S(1)} %copy-done) | data formatting | bytes 1572864
  (3 shorter events, 0.1 us)
Async XLA Ops:
  38.4 2.2 %copy-start.2 = (bf16[192,2048]{1,0:T(8,128)(2,1)S(1)}, bf16[192,2048]{1,0:T(8,128)(2,1)}, u32[]{:S(2)}) copy-start(bf16[192,2048]{1,0:T(8,128)(2,1)} %get-tuple-element.15) | copy-start | bytes 2359300
  40.6 1.4 %copy-start.1 = (bf16[192,2048]{1,0:T(8,128)(2,1)S(1)}, bf16[192,2048]{1,0:T(8,128)(2,1)}, u32[]{:S(2)}) copy-start(bf16[192,2048]{1,0:T(8,128)(2,1)} %get-tuple-element.16) | copy-start | bytes 2359300
  42.0 1.4 %copy-start = (bf16[192,2048]{1,0:T(8,128)(2,1)S(1)}, bf16[192,2048]{1,0:T(8,128)(2,1)}, u32[]{:S(2)}) copy-start(bf16[192,2048]{1,0:T(8,128)(2,1)} %get-tuple-element.17) | copy-start | bytes 2359300

commit v4 on v3

--- a/solution.py
+++ b/solution.py
@@ -248,7 +248,7 @@
     bf16, f32 = jnp.bfloat16, jnp.float32
     return pl.pallas_call(
         functools.partial(kernel, shards),
-        in_specs=[pl.BlockSpec(memory_space=pl.ANY)] * 4 + [vmem],
+        in_specs=[pl.BlockSpec(memory_space=pltpu.HBM)] * 4 + [vmem],
         out_specs=[vmem] * 4,
         out_shape=[jax.ShapeDtypeStruct((rows, feats), bf16)] * 4,
         scratch_shapes=[
@@ -281,7 +281,7 @@
             pltpu.SemaphoreType.DMA((4,)),
         ],
         compiler_params=pltpu.CompilerParams(
-            vmem_limit_bytes=56 * 1024 * 1024, collective_id=0, has_side_effects=True
+            vmem_limit_bytes=51 * 1024 * 1024, collective_id=0, has_side_effects=True
         ),
         cost_estimate=pl.CostEstimate(
             flops=10 * rows * columns * feats,

time: 45 us -> 41 us (0.911)
  local copies, waits for them, and re-layouts: 6.5 us -> 4.07 us
  Pallas kernels: 36.2 us -> 34.7 us
    unnamed x10 -> x6, local copies, waits for them, and re-layouts: 5.88 us -> 4.06 us
    pallas_call x1, Pallas kernels: 36.2 us -> 34.7 us  [attention(): pl.pallas_call(functools.partial(kernel, shards), in_specs=[pl.BlockSpec(...]
    reshape x1, local copies, waits for them, and re-layouts: 0.62 us -> 0.02 us  [body(): own_slots.reshape(-1, HEAD_DIM)]
where the time goes in v4:
time: 41 us; the launch traced here: 40.4 us
  Pallas kernels  34.7 us (85%)
  local copies, waits for them, and re-layouts  4.07 us (10%)
  other arithmetic  0.94 us (2%)
  between operations  0.69 us (2%)
    pallas_call x1, Pallas kernels, attention(): pl.pallas_call(functools.partial(kernel, shards), in_specs=[pl.BlockSpec(...  34.7 us
    unnamed x6, local copies, waits for them, and re-layouts  4.06 us
    select_n x1, other arithmetic, body(): jnp.where(i < rows, lax.dynamic_slice_in_dim(array, jnp.minimum(i, rows -...  0.86 us

profile of v4, /device:TPU:1, one launch (start us, length us, event | category | flops | bytes accessed | tf_op | source)
XLA Modules:
  0.0 40.4 jit_solution(17281783886931783185)
XLA Ops:
  0.7 0.9 %broadcast_select_fusion.2 = (bf16[1,2048]{1,0:T(2,128)(2,1)S(1)}, bf16[1,2048]{1,0:T(2,128)(2,1)S(1)}, bf16[1,2048]{1,0:T(2,128)(2,1)S(1)}, bf16[1,2048]{1,0:T(2,128)(2,1)S(1)}) fusion(pred[]{:T(512)S(6)} %lt.23, bf16[192,2048]{1,0:T(8,128)(2,1)} %v_in.1, s32[]{:T(128)S(6)} %select_n.39, s32[]{:T(128)S(6)} %select_n.42, pred[]{:T(512)S(6)} %lt.25, ...), kind=kLoop, calls=%fused_computation.3 | loop fusion | flops 8192 | bytes 32778 | tf_op jit(solution)/shard_map/jit(_where)/select_n | solution.py:301
  1.6 34.7 %shard_map.75 = (bf16[192,2048]{1,0:T(8,128)(2,1)S(1)}, bf16[192,2048]{1,0:T(8,128)(2,1)S(1)}, bf16[192,2048]{1,0:T(8,128)(2,1)S(1)}, bf16[192,2048]{1,0:T(8,128)(2,1)}) custom-call(bf16[192,2048]{1,0:T(8,128)(2,1)} %q_in.1, bf16[192,2048]{1,0:T(8,128)(2,1)} %k_in.1, bf16[192,2048]{1,0:T(8,128)(2,1)} %v_in.1, bf16[192,2048]{1,0:T(8,128)(2,1)} %g_in.1, ...), custom_call_target="tpu_custom_call" | custom-call | flops 1258291200 | bytes 9437184 | tf_op jit(solution)/shard_map/pallas_call | solution.py:249
  36.4 0.9 %copy.12 = bf16[192,2048]{1,0:T(8,128)(2,1)} copy(bf16[192,2048]{1,0:T(8,128)(2,1)S(1)} %get-tuple-element.14) | data formatting | bytes 1572864
  37.3 0.9 %copy.13 = bf16[192,2048]{1,0:T(8,128)(2,1)} copy(bf16[192,2048]{1,0:T(8,128)(2,1)S(1)} %get-tuple-element.15) | data formatting | bytes 1572864
  38.1 0.0 copy-start
  38.2 0.9 %copy.14 = bf16[192,2048]{1,0:T(8,128)(2,1)} copy(bf16[192,2048]{1,0:T(8,128)(2,1)S(1)} %get-tuple-element.16) | data formatting | bytes 1572864
  39.0 0.5 %copy-done = bf16[192,2048]{1,0:T(8,128)(2,1)S(1)} copy-done((bf16[192,2048]{1,0:T(8,128)(2,1)S(1)}, bf16[192,2048]{1,0:T(8,128)(2,1)}, u32[]{:S(2)}) %copy-start) | copy-done | bytes 786456
  39.6 0.9 %copy.15 = bf16[192,2048]{1,0:T(8,128)(2,1)} copy(bf16[192,2048]{1,0:T(8,128)(2,1)S(1)} %copy-done) | data formatting | bytes 1572864
  (4 shorter events, 0.1 us)
Async XLA Ops:
  38.1 1.4 %copy-start = (bf16[192,2048]{1,0:T(8,128)(2,1)S(1)}, bf16[192,2048]{1,0:T(8,128)(2,1)}, u32[]{:S(2)}) copy-start(bf16[192,2048]{1,0:T(8,128)(2,1)} %get-tuple-element.17) | copy-start | bytes 2359300

commit v5 on v4

--- a/solution.py
+++ b/solution.py
@@ -14,7 +14,7 @@
 OFF = 32
 TAIL = 96
 SLOT_DEV = 2
-HEADS_STEP = 4
+HEADS_STEP = 8
 SCALE = 1.0 / math.sqrt(HEAD_DIM)
 NEG = -1e30
 

time: 41 us -> 41.6 us (1.015)
  Pallas kernels: 34.7 us -> 35.3 us
    pallas_call x1, Pallas kernels: 34.7 us -> 35.3 us  [attention(): pl.pallas_call(functools.partial(kernel, shards), in_specs=[pl.BlockSpec(...]
where the time goes in v5:
time: 41.6 us; the launch traced here: 41 us
  Pallas kernels  35.3 us (85%)
  local copies, waits for them, and re-layouts  4.07 us (10%)
  other arithmetic  0.94 us (2%)
  between operations  0.69 us (2%)
    pallas_call x1, Pallas kernels, attention(): pl.pallas_call(functools.partial(kernel, shards), in_specs=[pl.BlockSpec(...  35.3 us
    unnamed x6, local copies, waits for them, and re-layouts  4.06 us
    select_n x1, other arithmetic, body(): jnp.where(i < rows, lax.dynamic_slice_in_dim(array, jnp.minimum(i, rows -...  0.86 us

profile of v5, /device:TPU:1, one launch (start us, length us, event | category | flops | bytes accessed | tf_op | source)
XLA Modules:
  0.0 41.0 jit_solution(6687070600678280217)
XLA Ops:
  0.7 0.9 %broadcast_select_fusion.2 = (bf16[1,2048]{1,0:T(2,128)(2,1)S(1)}, bf16[1,2048]{1,0:T(2,128)(2,1)S(1)}, bf16[1,2048]{1,0:T(2,128)(2,1)S(1)}, bf16[1,2048]{1,0:T(2,128)(2,1)S(1)}) fusion(pred[]{:T(512)S(6)} %lt.23, bf16[192,2048]{1,0:T(8,128)(2,1)} %v_in.1, s32[]{:T(128)S(6)} %select_n.39, s32[]{:T(128)S(6)} %select_n.42, pred[]{:T(512)S(6)} %lt.25, ...), kind=kLoop, calls=%fused_computation.3 | loop fusion | flops 8192 | bytes 32778 | tf_op jit(solution)/shard_map/jit(_where)/select_n | solution.py:301
  1.6 35.3 %shard_map.75 = (bf16[192,2048]{1,0:T(8,128)(2,1)S(1)}, bf16[192,2048]{1,0:T(8,128)(2,1)S(1)}, bf16[192,2048]{1,0:T(8,128)(2,1)S(1)}, bf16[192,2048]{1,0:T(8,128)(2,1)}) custom-call(bf16[192,2048]{1,0:T(8,128)(2,1)} %q_in.1, bf16[192,2048]{1,0:T(8,128)(2,1)} %k_in.1, bf16[192,2048]{1,0:T(8,128)(2,1)} %v_in.1, bf16[192,2048]{1,0:T(8,128)(2,1)} %g_in.1, ...), custom_call_target="tpu_custom_call" | custom-call | flops 1258291200 | bytes 9437184 | tf_op jit(solution)/shard_map/pallas_call | solution.py:249
  37.0 0.9 %copy.12 = bf16[192,2048]{1,0:T(8,128)(2,1)} copy(bf16[192,2048]{1,0:T(8,128)(2,1)S(1)} %get-tuple-element.14) | data formatting | bytes 1572864
  37.8 0.9 %copy.13 = bf16[192,2048]{1,0:T(8,128)(2,1)} copy(bf16[192,2048]{1,0:T(8,128)(2,1)S(1)} %get-tuple-element.15) | data formatting | bytes 1572864
  38.7 0.0 copy-start
  38.7 0.9 %copy.14 = bf16[192,2048]{1,0:T(8,128)(2,1)} copy(bf16[192,2048]{1,0:T(8,128)(2,1)S(1)} %get-tuple-element.16) | data formatting | bytes 1572864
  39.6 0.5 %copy-done = bf16[192,2048]{1,0:T(8,128)(2,1)S(1)} copy-done((bf16[192,2048]{1,0:T(8,128)(2,1)S(1)}, bf16[192,2048]{1,0:T(8,128)(2,1)}, u32[]{:S(2)}) %copy-start) | copy-done | bytes 786456
  40.1 0.9 %copy.15 = bf16[192,2048]{1,0:T(8,128)(2,1)} copy(bf16[192,2048]{1,0:T(8,128)(2,1)S(1)} %copy-done) | data formatting | bytes 1572864
  (4 shorter events, 0.1 us)
Async XLA Ops:
  38.7 1.4 %copy-start = (bf16[192,2048]{1,0:T(8,128)(2,1)S(1)}, bf16[192,2048]{1,0:T(8,128)(2,1)}, u32[]{:S(2)}) copy-start(bf16[192,2048]{1,0:T(8,128)(2,1)} %get-tuple-element.17) | copy-start | bytes 2359300

commit v6 on v4

--- a/solution.py
+++ b/solution.py
@@ -67,7 +67,7 @@
 
 
 def kernel(shards, q_in, k_in, v_in, g_in, mine_ref, out_ref, qg_ref, key_ref, value_ref,
-           q_ref, k_ref, v_ref, g_ref, kg_ref, vg_ref, after_ref, sum_ref, bias_ref, halo_ref, hg_ref, slot_ref, part_ref, got_ref, ks_ref, vs_ref,
+           q_ref, k_ref, v_ref, g_ref, kg_ref, vg_ref, after_ref, sum_ref, early_ref, late_ref, halo_ref, hg_ref, slot_ref, part_ref, got_ref, ks_ref, vs_ref,
            kp_ref, vp_ref, halo_send, halo_recv, slot_send, slot_recv, back_send, back_recv,
            part_send, part_recv, load_sem):
     rows, feats = q_ref.shape
@@ -154,8 +154,10 @@
             each(0, steps, send)
 
     local, summary = bias_of(me, rows, slots)
-    bias_ref[:, : TAIL + rows] = local
-    bias_ref[:, TAIL + rows :] = summary
+    early_ref[:, : 2 * TAIL] = local[:TAIL, : 2 * TAIL]
+    early_ref[:, 2 * TAIL :] = summary[:TAIL]
+    late_ref[:, : rows - OFF] = local[TAIL:, TAIL + OFF :]
+    late_ref[:, rows - OFF :] = summary[TAIL:]
 
     each(0, me, lambda p: slot_copy(p, p).wait_recv())
 
@@ -177,15 +179,22 @@
             of_head = pl.ds(h, slots, stride=HEADS)
             k_slots = ks_ref[of_head, :].astype(jnp.bfloat16)
             v_slots = vs_ref[of_head, :].astype(jnp.bfloat16)
-            k = jnp.concatenate([halo_ref[0, :, c], k_ref[:, c], k_slots], axis=0)
-            v = jnp.concatenate([halo_ref[1, :, c], v_ref[:, c], v_slots], axis=0)
-            attended, qgrad, kg, vg = one_head(q_ref[:, c], k, v, g_ref[:, c], bias_ref[...])
-            out_ref[:, c] = attended
-            qg_ref[:, c] = qgrad
-            for n, (grad, own_ref, term_ref) in enumerate(((kg, kg_ref, kp_ref), (vg, vg_ref, vp_ref))):
-                hg_ref[n, :, c] = grad[:TAIL].astype(jnp.bfloat16)
-                own_ref[:, c] = grad[TAIL : TAIL + rows]
-                term_ref[of_head, :] = grad[TAIL + rows :]
+            k = jnp.concatenate([halo_ref[0, :, c], k_ref[:TAIL, c], k_slots], axis=0)
+            v = jnp.concatenate([halo_ref[1, :, c], v_ref[:TAIL, c], v_slots], axis=0)
+            out_ref[:TAIL, c], qg_ref[:TAIL, c], *early = one_head(
+                q_ref[:TAIL, c], k, v, g_ref[:TAIL, c], early_ref[...]
+            )
+            k = jnp.concatenate([k_ref[OFF:, c], k_slots], axis=0)
+            v = jnp.concatenate([v_ref[OFF:, c], v_slots], axis=0)
+            out_ref[TAIL:, c], qg_ref[TAIL:, c], *late = one_head(
+                q_ref[TAIL:, c], k, v, g_ref[TAIL:, c], late_ref[...]
+            )
+            for n, (own_ref, term_ref) in enumerate(((kg_ref, kp_ref), (vg_ref, vp_ref))):
+                hg_ref[n, :, c] = early[n][:TAIL].astype(jnp.bfloat16)
+                own_ref[:OFF, c] = early[n][TAIL : TAIL + OFF]
+                own_ref[OFF:TAIL, c] = early[n][TAIL + OFF : 2 * TAIL] + late[n][: TAIL - OFF]
+                own_ref[TAIL:, c] = late[n][TAIL - OFF : rows - OFF]
+                term_ref[of_head, :] = early[n][2 * TAIL :] + late[n][rows - OFF :]
         for size, fits in ways:
             @pl.when((me > 0) & fits(lead))
             def _():
@@ -260,7 +269,8 @@
             pltpu.VMEM((rows, feats), f32),
             pltpu.VMEM((2, TAIL, feats), bf16),
             pltpu.VMEM((2 * half, HEAD_DIM), f32),
-            pltpu.VMEM((rows, columns), f32),
+            pltpu.VMEM((TAIL, 2 * TAIL + slots), f32),
+            pltpu.VMEM((rows - TAIL, rows - OFF + slots), f32),
             pltpu.VMEM((2, TAIL, feats), bf16),
             pltpu.VMEM((2, TAIL, feats), bf16),
             pltpu.VMEM((shards, 2 * half, HEAD_DIM), bf16),

time: 41 us -> 50.1 us (1.22)
  Pallas kernels: 34.7 us -> 43.8 us
    pallas_call x1, Pallas kernels: 34.7 us -> 43.8 us  [attention(): pl.pallas_call(functools.partial(kernel, shards), in_specs=[pl.BlockSpec(...]
where the time goes in v6:
time: 50.1 us; the launch traced here: 49.5 us
  Pallas kernels  43.8 us (87%)
  local copies, waits for them, and re-layouts  4.07 us (8%)
  other arithmetic  0.94 us (2%)
  between operations  0.69 us (1%)
    pallas_call x1, Pallas kernels, attention(): pl.pallas_call(functools.partial(kernel, shards), in_specs=[pl.BlockSpec(...  43.8 us
    unnamed x6, local copies, waits for them, and re-layouts  4.06 us

profile of v6, /device:TPU:1, one launch (start us, length us, event | category | flops | bytes accessed | tf_op | source)
XLA Modules:
  0.0 49.5 jit_solution(15279242550173209649)
XLA Ops:
  0.7 0.9 %broadcast_select_fusion.2 = (bf16[1,2048]{1,0:T(2,128)(2,1)S(1)}, bf16[1,2048]{1,0:T(2,128)(2,1)S(1)}, bf16[1,2048]{1,0:T(2,128)(2,1)S(1)}, bf16[1,2048]{1,0:T(2,128)(2,1)S(1)}) fusion(pred[]{:T(512)S(6)} %lt.23, bf16[192,2048]{1,0:T(8,128)(2,1)} %v_in.1, s32[]{:T(128)S(6)} %select_n.39, s32[]{:T(128)S(6)} %select_n.42, pred[]{:T(512)S(6)} %lt.25, ...), kind=kLoop, calls=%fused_computation.3 | loop fusion | flops 8192 | bytes 32778 | tf_op jit(solution)/shard_map/jit(_where)/select_n | solution.py:311
  1.6 43.8 %shard_map.75 = (bf16[192,2048]{1,0:T(8,128)(2,1)S(1)}, bf16[192,2048]{1,0:T(8,128)(2,1)S(1)}, bf16[192,2048]{1,0:T(8,128)(2,1)S(1)}, bf16[192,2048]{1,0:T(8,128)(2,1)}) custom-call(bf16[192,2048]{1,0:T(8,128)(2,1)} %q_in.1, bf16[192,2048]{1,0:T(8,128)(2,1)} %k_in.1, bf16[192,2048]{1,0:T(8,128)(2,1)} %v_in.1, bf16[192,2048]{1,0:T(8,128)(2,1)} %g_in.1, ...), custom_call_target="tpu_custom_call" | custom-call | flops 1258291200 | bytes 9437184 | tf_op jit(solution)/shard_map/pallas_call | solution.py:258
  45.5 0.9 %copy.12 = bf16[192,2048]{1,0:T(8,128)(2,1)} copy(bf16[192,2048]{1,0:T(8,128)(2,1)S(1)} %get-tuple-element.14) | data formatting | bytes 1572864
  46.4 0.9 %copy.13 = bf16[192,2048]{1,0:T(8,128)(2,1)} copy(bf16[192,2048]{1,0:T(8,128)(2,1)S(1)} %get-tuple-element.15) | data formatting | bytes 1572864
  47.2 0.0 copy-start
  47.2 0.9 %copy.14 = bf16[192,2048]{1,0:T(8,128)(2,1)} copy(bf16[192,2048]{1,0:T(8,128)(2,1)S(1)} %get-tuple-element.16) | data formatting | bytes 1572864
  48.1 0.5 %copy-done = bf16[192,2048]{1,0:T(8,128)(2,1)S(1)} copy-done((bf16[192,2048]{1,0:T(8,128)(2,1)S(1)}, bf16[192,2048]{1,0:T(8,128)(2,1)}, u32[]{:S(2)}) %copy-start) | copy-done | bytes 786456
  48.7 0.9 %copy.15 = bf16[192,2048]{1,0:T(8,128)(2,1)} copy(bf16[192,2048]{1,0:T(8,128)(2,1)S(1)} %copy-done) | data formatting | bytes 1572864
  (4 shorter events, 0.1 us)
Async XLA Ops:
  47.2 1.4 %copy-start = (bf16[192,2048]{1,0:T(8,128)(2,1)S(1)}, bf16[192,2048]{1,0:T(8,128)(2,1)}, u32[]{:S(2)}) copy-start(bf16[192,2048]{1,0:T(8,128)(2,1)} %get-tuple-element.17) | copy-start | bytes 2359300

commit v7 on v6

--- a/solution.py
+++ b/solution.py
@@ -46,17 +46,26 @@
 TN = ((0,), (0,))
 
 
-def one_head(q, k, v, g, bias):
-    scores = dot(q, k, NT) * SCALE + bias
-    top = jnp.max(scores, axis=1, keepdims=True)
-    expo = jnp.exp(scores - top)
-    prob = expo * (1.0 / jnp.sum(expo, axis=1, keepdims=True))
-    weights = prob.astype(jnp.bfloat16)
-    attended = dot(weights, v, NN).astype(jnp.bfloat16)
-    delta = jnp.sum(g.astype(jnp.float32) * attended.astype(jnp.float32), axis=1, keepdims=True)
-    dscores = (prob * (dot(g, v, NT) - delta)).astype(jnp.bfloat16)
-    qgrad = (dot(dscores, k, NN) * SCALE).astype(jnp.bfloat16)
-    return attended, qgrad, dot(dscores, q, TN) * SCALE, dot(weights, g, TN)
+def all_chains(chains):
+    scores = [dot(q, k, NT) * SCALE + bias for q, k, v, g, bias in chains]
+    dweights = [dot(g, v, NT) for q, k, v, g, bias in chains]
+    tops = [jnp.max(x, axis=1, keepdims=True) for x in scores]
+    expos = [jnp.exp(x - top) for x, top in zip(scores, tops)]
+    totals = [jnp.sum(x, axis=1, keepdims=True) for x in expos]
+    probs = [x * (1.0 / total) for x, total in zip(expos, totals)]
+    weights = [x.astype(jnp.bfloat16) for x in probs]
+    attended = [dot(w, c[2], NN).astype(jnp.bfloat16) for w, c in zip(weights, chains)]
+    vgrads = [dot(w, c[3], TN) for w, c in zip(weights, chains)]
+    deltas = [
+        jnp.sum(c[3].astype(jnp.float32) * x.astype(jnp.float32), axis=1, keepdims=True)
+        for x, c in zip(attended, chains)
+    ]
+    dscores = [
+        (p * (dw - delta)).astype(jnp.bfloat16) for p, dw, delta in zip(probs, dweights, deltas)
+    ]
+    qgrads = [(dot(ds, c[1], NN) * SCALE).astype(jnp.bfloat16) for ds, c in zip(dscores, chains)]
+    kgrads = [dot(ds, c[0], TN) * SCALE for ds, c in zip(dscores, chains)]
+    return list(zip(attended, qgrads, kgrads, vgrads))
 
 
 def remote(src, dst, send, recv, seq):
@@ -173,22 +182,25 @@
             def _():
                 for i in range(2):
                     halo_copy(i, j, size).wait_recv()
+        chains = []
+        places = []
         for i in range(HEADS_STEP):
             h = j * HEADS_STEP + i
             c = pl.ds(pl.multiple_of(h * HEAD_DIM, HEAD_DIM), HEAD_DIM)
             of_head = pl.ds(h, slots, stride=HEADS)
+            places.append((c, of_head))
             k_slots = ks_ref[of_head, :].astype(jnp.bfloat16)
             v_slots = vs_ref[of_head, :].astype(jnp.bfloat16)
             k = jnp.concatenate([halo_ref[0, :, c], k_ref[:TAIL, c], k_slots], axis=0)
             v = jnp.concatenate([halo_ref[1, :, c], v_ref[:TAIL, c], v_slots], axis=0)
-            out_ref[:TAIL, c], qg_ref[:TAIL, c], *early = one_head(
-                q_ref[:TAIL, c], k, v, g_ref[:TAIL, c], early_ref[...]
-            )
+            chains.append((q_ref[:TAIL, c], k, v, g_ref[:TAIL, c], early_ref[...]))
             k = jnp.concatenate([k_ref[OFF:, c], k_slots], axis=0)
             v = jnp.concatenate([v_ref[OFF:, c], v_slots], axis=0)
-            out_ref[TAIL:, c], qg_ref[TAIL:, c], *late = one_head(
-                q_ref[TAIL:, c], k, v, g_ref[TAIL:, c], late_ref[...]
-            )
+            chains.append((q_ref[TAIL:, c], k, v, g_ref[TAIL:, c], late_ref[...]))
+        results = all_chains(chains)
+        for i, (c, of_head) in enumerate(places):
+            out_ref[:TAIL, c], qg_ref[:TAIL, c], *early = results[2 * i]
+            out_ref[TAIL:, c], qg_ref[TAIL:, c], *late = results[2 * i + 1]
             for n, (own_ref, term_ref) in enumerate(((kg_ref, kp_ref), (vg_ref, vp_ref))):
                 hg_ref[n, :, c] = early[n][:TAIL].astype(jnp.bfloat16)
                 own_ref[:OFF, c] = early[n][TAIL : TAIL + OFF]

time: 50.1 us -> 33.7 us (0.67)
  Pallas kernels: 43.8 us -> 27.5 us
    pallas_call x1, Pallas kernels: 43.8 us -> 27.5 us  [attention(): pl.pallas_call(functools.partial(kernel, shards), in_specs=[pl.BlockSpec(...]
where the time goes in v7:
time: 33.7 us; the launch traced here: 33.2 us
  Pallas kernels  27.5 us (82%)
  local copies, waits for them, and re-layouts  4.07 us (12%)
  other arithmetic  0.94 us (3%)
  between operations  0.69 us (2%)
    pallas_call x1, Pallas kernels, attention(): pl.pallas_call(functools.partial(kernel, shards), in_specs=[pl.BlockSpec(...  27.5 us
    unnamed x6, local copies, waits for them, and re-layouts  4.06 us
    select_n x1, other arithmetic, body(): jnp.where(i < rows, lax.dynamic_slice_in_dim(array, jnp.minimum(i, rows -...  0.86 us

profile of v7, /device:TPU:1, one launch (start us, length us, event | category | flops | bytes accessed | tf_op | source)
XLA Modules:
  0.0 33.2 jit_solution(3215777365188429793)
XLA Ops:
  0.7 0.9 %broadcast_select_fusion.2 = (bf16[1,2048]{1,0:T(2,128)(2,1)S(1)}, bf16[1,2048]{1,0:T(2,128)(2,1)S(1)}, bf16[1,2048]{1,0:T(2,128)(2,1)S(1)}, bf16[1,2048]{1,0:T(2,128)(2,1)S(1)}) fusion(pred[]{:T(512)S(6)} %lt.23, bf16[192,2048]{1,0:T(8,128)(2,1)} %v_in.1, s32[]{:T(128)S(6)} %select_n.39, s32[]{:T(128)S(6)} %select_n.42, pred[]{:T(512)S(6)} %lt.25, ...), kind=kLoop, calls=%fused_computation.3 | loop fusion | flops 8192 | bytes 32778 | tf_op jit(solution)/shard_map/jit(_where)/select_n | solution.py:323
  1.6 27.5 %shard_map.75 = (bf16[192,2048]{1,0:T(8,128)(2,1)S(1)}, bf16[192,2048]{1,0:T(8,128)(2,1)S(1)}, bf16[192,2048]{1,0:T(8,128)(2,1)S(1)}, bf16[192,2048]{1,0:T(8,128)(2,1)}) custom-call(bf16[192,2048]{1,0:T(8,128)(2,1)} %q_in.1, bf16[192,2048]{1,0:T(8,128)(2,1)} %k_in.1, bf16[192,2048]{1,0:T(8,128)(2,1)} %v_in.1, bf16[192,2048]{1,0:T(8,128)(2,1)} %g_in.1, ...), custom_call_target="tpu_custom_call" | custom-call | flops 1258291200 | bytes 9437184 | tf_op jit(solution)/shard_map/pallas_call | solution.py:270
  29.1 0.9 %copy.12 = bf16[192,2048]{1,0:T(8,128)(2,1)} copy(bf16[192,2048]{1,0:T(8,128)(2,1)S(1)} %get-tuple-element.14) | data formatting | bytes 1572864
  30.0 0.9 %copy.13 = bf16[192,2048]{1,0:T(8,128)(2,1)} copy(bf16[192,2048]{1,0:T(8,128)(2,1)S(1)} %get-tuple-element.15) | data formatting | bytes 1572864
  30.9 0.0 copy-start
  30.9 0.9 %copy.14 = bf16[192,2048]{1,0:T(8,128)(2,1)} copy(bf16[192,2048]{1,0:T(8,128)(2,1)S(1)} %get-tuple-element.16) | data formatting | bytes 1572864
  31.8 0.5 %copy-done = bf16[192,2048]{1,0:T(8,128)(2,1)S(1)} copy-done((bf16[192,2048]{1,0:T(8,128)(2,1)S(1)}, bf16[192,2048]{1,0:T(8,128)(2,1)}, u32[]{:S(2)}) %copy-start) | copy-done | bytes 786456
  32.3 0.9 %copy.15 = bf16[192,2048]{1,0:T(8,128)(2,1)} copy(bf16[192,2048]{1,0:T(8,128)(2,1)S(1)} %copy-done) | data formatting | bytes 1572864
  (4 shorter events, 0.1 us)
Async XLA Ops:
  30.9 1.4 %copy-start = (bf16[192,2048]{1,0:T(8,128)(2,1)S(1)}, bf16[192,2048]{1,0:T(8,128)(2,1)}, u32[]{:S(2)}) copy-start(bf16[192,2048]{1,0:T(8,128)(2,1)} %get-tuple-element.17) | copy-start | bytes 2359300

commit v8 on v7

--- a/solution.py
+++ b/solution.py
@@ -14,7 +14,7 @@
 OFF = 32
 TAIL = 96
 SLOT_DEV = 2
-HEADS_STEP = 4
+HEADS_STEP = 8
 SCALE = 1.0 / math.sqrt(HEAD_DIM)
 NEG = -1e30
 
@@ -303,7 +303,7 @@
             pltpu.SemaphoreType.DMA((4,)),
         ],
         compiler_params=pltpu.CompilerParams(
-            vmem_limit_bytes=51 * 1024 * 1024, collective_id=0, has_side_effects=True
+            vmem_limit_bytes=51700 * 1024, collective_id=0, has_side_effects=True
         ),
         cost_estimate=pl.CostEstimate(
             flops=10 * rows * columns * feats,

time: 33.7 us -> 33.1 us (0.982)
  local copies, waits for them, and re-layouts: 4.07 us -> 3.54 us
    unnamed x6 -> x4, local copies, waits for them, and re-layouts: 4.06 us -> 3.52 us
where the time goes in v8:
time: 33.1 us; the launch traced here: 32.6 us
  Pallas kernels  27.4 us (83%)
  local copies, waits for them, and re-layouts  3.54 us (11%)
  other arithmetic  0.94 us (3%)
  between operations  0.69 us (2%)
    pallas_call x1, Pallas kernels, attention(): pl.pallas_call(functools.partial(kernel, shards), in_specs=[pl.BlockSpec(...  27.4 us
    unnamed x4, local copies, waits for them, and re-layouts  3.52 us
    select_n x1, other arithmetic, body(): jnp.where(i < rows, lax.dynamic_slice_in_dim(array, jnp.minimum(i, rows -...  0.86 us

profile of v8, /device:TPU:1, one launch (start us, length us, event | category | flops | bytes accessed | tf_op | source)
XLA Modules:
  0.0 32.6 jit_solution(889150344152028147)
XLA Ops:
  0.7 0.9 %broadcast_select_fusion.2 = (bf16[1,2048]{1,0:T(2,128)(2,1)S(1)}, bf16[1,2048]{1,0:T(2,128)(2,1)S(1)}, bf16[1,2048]{1,0:T(2,128)(2,1)S(1)}, bf16[1,2048]{1,0:T(2,128)(2,1)S(1)}) fusion(pred[]{:T(512)S(6)} %lt.23, bf16[192,2048]{1,0:T(8,128)(2,1)} %v_in.1, s32[]{:T(128)S(6)} %select_n.39, s32[]{:T(128)S(6)} %select_n.42, pred[]{:T(512)S(6)} %lt.25, ...), kind=kLoop, calls=%fused_computation.3 | loop fusion | flops 8192 | bytes 32778 | tf_op jit(solution)/shard_map/jit(_where)/select_n | solution.py:323
  1.6 27.4 %shard_map.75 = (bf16[192,2048]{1,0:T(8,128)(2,1)S(1)}, bf16[192,2048]{1,0:T(8,128)(2,1)S(1)}, bf16[192,2048]{1,0:T(8,128)(2,1)S(1)}, bf16[192,2048]{1,0:T(8,128)(2,1)S(1)}) custom-call(bf16[192,2048]{1,0:T(8,128)(2,1)} %q_in.1, bf16[192,2048]{1,0:T(8,128)(2,1)} %k_in.1, bf16[192,2048]{1,0:T(8,128)(2,1)} %v_in.1, bf16[192,2048]{1,0:T(8,128)(2,1)} %g_in.1, ...), custom_call_target="tpu_custom_call" | custom-call | flops 1258291200 | bytes 9437184 | tf_op jit(solution)/shard_map/pallas_call | solution.py:270
  29.0 0.9 %copy.12 = bf16[192,2048]{1,0:T(8,128)(2,1)} copy(bf16[192,2048]{1,0:T(8,128)(2,1)S(1)} %get-tuple-element.14) | data formatting | bytes 1572864
  29.9 0.9 %copy.13 = bf16[192,2048]{1,0:T(8,128)(2,1)} copy(bf16[192,2048]{1,0:T(8,128)(2,1)S(1)} %get-tuple-element.15) | data formatting | bytes 1572864
  30.8 0.9 %copy.14 = bf16[192,2048]{1,0:T(8,128)(2,1)} copy(bf16[192,2048]{1,0:T(8,128)(2,1)S(1)} %get-tuple-element.16) | data formatting | bytes 1572864
  31.7 0.9 %copy.15 = bf16[192,2048]{1,0:T(8,128)(2,1)} copy(bf16[192,2048]{1,0:T(8,128)(2,1)S(1)} %get-tuple-element.17) | data formatting | bytes 1572864
  (4 shorter events, 0.1 us)
